TPU v7x, 128 devices: a whole 4x4x4 slice. The times are simulated.
128 devices in a mesh: section: 4 (over x), ctx: 32 (over z, y, core).
Axes of the slice: x: 4, y: 4, z: 4, core: 2. Of those that a mesh axis runs over, the one named last changes fastest.
Arguments:
- queries: bfloat16 [4, 4096, 4096], P('section', 'ctx'), may hold values from -135 to 135
- key_rows: bfloat16 [4, 4096, 512], P('section', 'ctx'), may hold values from -5.1 to 5.1
- value_rows: bfloat16 [4, 4096, 512], P('section', 'ctx'), may hold values from -6 to 6
- out_grad: bfloat16 [4, 4096, 4096], P('section', 'ctx'), may hold values from -6 to 6
- kv_weight: bfloat16 [4, 8192, 1024], P('section', 'ctx'), may hold values from -0.0625 to 0.0625
- doc_lengths: int32 [16], replicated, may hold values from 1 to 1024, 4096 in all
- block_plan: int32 [32], replicated, may hold values from 0 to 31, each once
Outputs:
- query_grad: bfloat16 [4, 4096, 4096], P('section', 'ctx')
- input_grad: bfloat16 [4, 4096, 8192], P('section', 'ctx')
Inputs may be any that keep to these rules, and one draw needn't show every extreme that they name: `doc_lengths`: the 16 lengths sum to 4096 and the largest is exactly 1024. `block_plan`: every block number appears exactly once.
All inputs are finite; a program needn't handle non-finite values.
Results may differ from a plain program's by a relative error of at most 0.014.
Values may be sent and summed in bfloat16 or wider, within the bound.
A program may use at most 128 MiB of HBM per device.

v0:
```python
import functools
import math

import jax
import jax.numpy as jnp
from jax import lax
from jax.experimental import pallas as pl
from jax.experimental.pallas import tpu as pltpu
from jax.sharding import PartitionSpec as P

HQ = 32
HK = 4
HD = 128
BLOCK = 128
GROUP = HQ // HK
BACK = 8
SLOTS = BACK + 1
CH = 2 * HK
SUB = 32
RG = BLOCK // SUB
MASKED = -1e30
MESH = pl.DeviceIdType.MESH


def rem(a, b):
    return lax.rem(a, b)


def div(a, b):
    return lax.div(a, b)


def kernel(
    n, sections, lens, plan, inv, q_hbm, k_ref, v_ref, o_hbm, w_hbm, dq_hbm, out_hbm,
    q_s, o_s, dq_s, kvw, recv1, send2, bias, dk_acc, dv_acc, part, recv3, kvo, kvg, wsh, wfull, outs,
    in_sem, dq_sem, s1s, s1r, s2s, s2r, s3s, s3r, xs, xr, gs, gr, os_, or_, loc_sem, wxs, wxr, wgs, wgr,
):
    me = lax.axis_index("ctx")
    sec = lax.axis_index("section")
    rg = div(me, CH)
    ch = rem(me, CH)
    before = rem(sec + sections - 1, sections)

    def remote(src, dst, send, recv, **where):
        return pltpu.make_async_remote_copy(
            src_ref=src, dst_ref=dst, send_sem=send, recv_sem=recv,
            device_id=where, device_id_type=MESH,
        )

    def rows(group):
        return pl.ds(pl.multiple_of(group * SUB, SUB), SUB)

    def others(body):
        def step(k, carry):
            body(rem(me + k, n))
            return carry
        lax.fori_loop(1, n, step, 0)

    load_q = pltpu.make_async_copy(q_hbm, q_s, in_sem.at[0])
    load_o = pltpu.make_async_copy(o_hbm, o_s, in_sem.at[1])
    load_q.start()
    load_o.start()

    barrier = pltpu.get_barrier_semaphore()
    others(lambda j: pl.semaphore_signal(barrier, inc=1, device_id={"ctx": j}, device_id_type=MESH))
    pl.semaphore_signal(barrier, inc=1, device_id={"section": rem(sec + 1, sections)}, device_id_type=MESH)
    for head in range(HK):
        kvw[head, BACK] = k_ref[:, head * HD:(head + 1) * HD]
        kvw[HK + head, BACK] = v_ref[:, head * HD:(head + 1) * HD]
    pl.semaphore_wait(barrier, n)

    def piece_out(j):
        return remote(kvw.at[rem(j, CH), BACK, rows(div(j, CH))], recv1.at[me], s1s.at[j], s1r.at[me], ctx=j)

    others(lambda j: piece_out(j).start())
    w_shift = remote(w_hbm, wsh, wxs, wxr, section=before)
    w_shift.start()
    recv1[me] = kvw[ch, BACK, rows(rg)]

    token_block = plan[me]
    row_token = token_block * BLOCK + lax.broadcasted_iota(jnp.int32, (1, BLOCK), 1)
    start = jnp.zeros((1, BLOCK), jnp.int32)
    end = jnp.int32(0)
    for j in range(lens.shape[0]):
        end = end + lens[j]
        start = jnp.where(row_token >= end, end, start)
    key_token = (token_block - BACK) * BLOCK + lax.broadcasted_iota(jnp.int32, (SLOTS * BLOCK, BLOCK), 0)
    seen = jnp.logical_and(key_token >= start, key_token <= row_token)
    bias[...] = jnp.where(seen, 0.0, MASKED)

    def piece_in(j):
        return remote(kvw.at[0, BACK, rows(0)], recv1.at[j], s1s.at[j], s1r.at[j], ctx=j)

    others(lambda j: piece_in(j).wait_recv())

    def window_out(d):
        return remote(send2.at[d], kvw.at[ch, pl.ds(0, BACK), rows(rg)], s2s.at[d], s2r.at[me], ctx=d)

    def window_send(d):
        first = plan[d] - BACK
        for w in range(BACK):
            send2[d, w] = recv1[inv[jnp.maximum(first + w, 0)]]
        window_out(d).start()

    others(window_send)
    for w in range(BACK):
        kvw[ch, w, rows(rg)] = recv1[inv[jnp.maximum(token_block - BACK + w, 0)]]

    def window_in(j):
        return remote(send2.at[j], kvw.at[rem(j, CH), pl.ds(0, BACK), rows(div(j, CH))], s2s.at[j], s2r.at[j], ctx=j)

    others(lambda j: window_in(j).wait_recv())

    w_shift.wait_recv()
    w_slot = rem(me, RG)

    def w_rows(slot):
        return wfull.at[pl.ds(pl.multiple_of(slot * w_hbm.shape[0], 256), w_hbm.shape[0])]

    def w_target(z):
        return z * CH + div(me, RG)

    for z in range(RG):
        @pl.when(w_target(z) != me)
        def _():
            remote(wsh, w_rows(w_slot), wgs.at[z], wgr.at[w_slot], ctx=w_target(z)).start()

        @pl.when(w_target(z) == me)
        def _():
            pltpu.make_async_copy(wsh, w_rows(w_slot), loc_sem.at[1]).start()

    load_q.wait()
    load_o.wait()

    scale = 1.0 / math.sqrt(HD)
    power = scale * math.log2(math.e)
    nt = (((1,), (1,)), ((), ()))

    def part_out(j):
        return remote(part.at[rem(j, CH), :, rows(div(j, CH))], recv3.at[me], s3s.at[j], s3r.at[me], ctx=j)

    def part_own():
        return pltpu.make_async_copy(part.at[ch, :, rows(rg)], recv3.at[me], loc_sem.at[0])

    def one_head(step, carry):
        head = rem(step + me, HK)
        keys = kvw[head].reshape(SLOTS * BLOCK, HD)
        values = kvw[HK + head].reshape(SLOTS * BLOCK, HD)
        keys_t = keys.T

        def one_pair(pair, carry):
            def columns(i):
                return pl.ds(pl.multiple_of((head * GROUP + pair * 2 + i) * HD, HD), HD)

            q2 = jnp.concatenate([q_s[:, columns(0)], q_s[:, columns(1)]], axis=0)
            o2 = jnp.concatenate([o_s[:, columns(0)], o_s[:, columns(1)]], axis=0)
            b = bias[...]
            scores = lax.dot_general(keys, q2, nt, preferred_element_type=jnp.float32)
            scores = scores + jnp.concatenate([b, b], axis=1)
            grads = lax.dot_general(values, o2, nt, preferred_element_type=jnp.float32)
            peak = jnp.max(scores, axis=0, keepdims=True)
            terms = jnp.exp2((scores - peak) * power)
            inverse = 1.0 / jnp.sum(terms, axis=0, keepdims=True)
            delta = jnp.sum(terms * grads, axis=0, keepdims=True) * inverse
            prob = terms * inverse
            prob_low = prob.astype(jnp.bfloat16)
            score_low = (prob * (grads - delta)).astype(jnp.bfloat16)
            dv = jnp.dot(prob_low, o2, preferred_element_type=jnp.float32)
            dk = jnp.dot(score_low, q2, preferred_element_type=jnp.float32)
            dq_t = jnp.dot(keys_t, score_low, preferred_element_type=jnp.float32) * scale
            dq_s[:, columns(0)] = dq_t[:, :BLOCK].T.astype(jnp.bfloat16)
            dq_s[:, columns(1)] = dq_t[:, BLOCK:].T.astype(jnp.bfloat16)
            keep = jnp.where(pair == 0, 0.0, 1.0)
            dv_acc[...] = dv_acc[...] * keep + dv
            dk_acc[...] = dk_acc[...] * keep + dk
            return carry

        dv_acc[...] = jnp.zeros_like(dv_acc)
        dk_acc[...] = jnp.zeros_like(dk_acc)
        lax.fori_loop(0, GROUP // 2, one_pair, 0)
        part[head] = (dk_acc[...] * scale).astype(jnp.bfloat16).reshape(SLOTS, BLOCK, HD)
        part[HK + head] = dv_acc[...].astype(jnp.bfloat16).reshape(SLOTS, BLOCK, HD)

        def send(i, carry):
            j = div(i, 2) * CH + rem(i, 2) * HK + head

            @pl.when(j != me)
            def _():
                part_out(j).start()

            @pl.when(j == me)
            def _():
                part_own().start()
            return carry

        lax.fori_loop(0, 2 * RG, send, 0)
        wide = pl.ds(pl.multiple_of(head * GROUP * HD, GROUP * HD), GROUP * HD)
        pltpu.make_async_copy(dq_s.at[:, wide], dq_hbm.at[:, wide], dq_sem.at[head]).start()
        return carry

    lax.fori_loop(0, HK, one_head, 0)

    def part_in(j):
        return remote(part.at[0, :, rows(0)], recv3.at[j], s3s.at[j], s3r.at[j], ctx=j)

    others(lambda j: part_in(j).wait_recv())
    part_own().wait()

    per = n // RG

    def blocks(chunk):
        return pl.ds(pl.multiple_of(chunk * per, per), per)

    def x_copy(chunk):
        return remote(kvo.at[blocks(chunk)], kvg.at[ch, blocks(chunk)], xs.at[chunk], xr.at[chunk], section=before)

    def reduce_chunk(step, carry):
        chunk = rem(step + rg, RG)

        def one_block(i, carry):
            p = chunk * per + i
            total = jnp.zeros((SUB, HD), jnp.float32)
            for w in range(SLOTS):
                later = plan[p] + BACK - w
                term = recv3[inv[jnp.minimum(later, n - 1)], w].astype(jnp.float32)
                total = total + jnp.where(later < n, term, 0.0)
            kvo[p] = total.astype(jnp.bfloat16)
            return carry

        lax.fori_loop(0, per, one_block, 0)
        x_copy(chunk).start()
        return carry

    lax.fori_loop(0, RG, reduce_chunk, 0)

    def gather(chunk, source, target):
        return remote(
            kvg.at[source, blocks(chunk)], kvg.at[source, blocks(chunk)],
            gs.at[chunk, target], gr.at[chunk, source], ctx=rg * CH + target,
        )

    def gather_chunk(step, carry):
        chunk = rem(step + rg, RG)
        x_copy(chunk).wait_recv()
        for i in range(1, CH):
            gather(chunk, ch, rem(ch + i, CH)).start()
        return carry

    lax.fori_loop(0, RG, gather_chunk, 0)

    for u in range(RG):
        @pl.when(RG * ch + u != me)
        def _():
            remote(wsh, w_rows(u), wgs.at[u], wgr.at[u], ctx=RG * ch + u).wait_recv()

        @pl.when(RG * ch + u == me)
        def _():
            pltpu.make_async_copy(wsh, w_rows(u), loc_sem.at[1]).wait()

    wide = wfull.shape[0]

    def out_part(group, chunk):
        return out_hbm.at[rows(group), pl.ds(pl.multiple_of(chunk * wide, wide), wide)]

    def out_copy(p):
        return remote(outs.at[p], out_part(rg, ch), os_.at[p], or_.at[me], ctx=p)

    def out_own():
        return pltpu.make_async_copy(outs.at[me], out_part(rg, ch), loc_sem.at[2])

    def multiply_chunk(step, carry):
        chunk = rem(step + rg, RG)
        for i in range(1, CH):
            gather(chunk, rem(ch + i, CH), ch).wait_recv()
        left = jnp.concatenate([kvg[i, blocks(chunk)].reshape(per * SUB, HD) for i in range(CH)], axis=1)
        product = lax.dot_general(left, wfull[...], nt, preferred_element_type=jnp.float32)
        outs[blocks(chunk)] = product.astype(jnp.bfloat16).reshape(per, SUB, wide)

        def send(i, carry):
            p = chunk * per + rem(i + ch, per)

            @pl.when(p != me)
            def _():
                out_copy(p).start()

            @pl.when(p == me)
            def _():
                out_own().start()
            return carry

        lax.fori_loop(0, per, send, 0)
        return carry

    lax.fori_loop(0, RG, multiply_chunk, 0)

    others(lambda j: piece_out(j).wait_send())
    others(lambda j: window_out(j).wait_send())
    others(lambda j: part_out(j).wait_send())
    w_shift.wait_send()
    for z in range(RG):
        @pl.when(w_target(z) != me)
        def _():
            remote(wsh, w_rows(w_slot), wgs.at[z], wgr.at[w_slot], ctx=w_target(z)).wait_send()

    def sent(chunk, carry):
        x_copy(chunk).wait_send()
        for i in range(1, CH):
            gather(chunk, ch, rem(ch + i, CH)).wait_send()
        return carry

    lax.fori_loop(0, RG, sent, 0)
    for head in range(HK):
        wide_q = pl.ds(head * GROUP * HD, GROUP * HD)
        pltpu.make_async_copy(dq_s.at[:, wide_q], dq_hbm.at[:, wide_q], dq_sem.at[head]).wait()
    others(lambda j: out_copy(j).wait_send())
    out_own().wait()
    others(lambda j: remote(outs.at[j], out_part(div(j, CH), rem(j, CH)), os_.at[j], or_.at[j], ctx=j).wait_recv())


def shards(queries, key_rows, value_rows, out_grad, kv_weight, doc_lengths, block_plan):
    n = lax.axis_size("ctx")
    sections = lax.axis_size("section")
    number = jnp.arange(n, dtype=jnp.int32)
    inverse_plan = jnp.sum(jnp.where(block_plan[None, :] == number[:, None], number[None, :], 0), axis=1, dtype=jnp.int32)
    tokens, width = queries.shape[1:]
    features = kv_weight.shape[1]
    model = features * n
    share = model // CH
    per = n // RG
    smem = pl.BlockSpec(memory_space=pltpu.SMEM)
    vmem = pl.BlockSpec(memory_space=pltpu.VMEM)
    hbm = pl.BlockSpec(memory_space=pl.ANY)
    low = jnp.bfloat16
    dma = pltpu.SemaphoreType.DMA
    query_grad, input_grad = pl.pallas_call(
        functools.partial(kernel, n, sections),
        out_shape=(
            jax.ShapeDtypeStruct((tokens, width), low),
            jax.ShapeDtypeStruct((tokens, model), low),
        ),
        in_specs=[smem, smem, smem, hbm, vmem, vmem, hbm, hbm],
        out_specs=(hbm, hbm),
        scratch_shapes=[
            pltpu.VMEM((tokens, width), low),
            pltpu.VMEM((tokens, width), low),
            pltpu.VMEM((tokens, width), low),
            pltpu.VMEM((CH, SLOTS, BLOCK, HD), low),
            pltpu.VMEM((n, SUB, HD), low),
            pltpu.VMEM((n, BACK, SUB, HD), low),
            pltpu.VMEM((SLOTS * BLOCK, BLOCK), jnp.float32),
            pltpu.VMEM((SLOTS * BLOCK, HD), jnp.float32),
            pltpu.VMEM((SLOTS * BLOCK, HD), jnp.float32),
            pltpu.VMEM((CH, SLOTS, BLOCK, HD), low),
            pltpu.VMEM((n, SLOTS, SUB, HD), low),
            pltpu.VMEM((n, SUB, HD), low),
            pltpu.VMEM((CH, n, SUB, HD), low),
            pltpu.VMEM((features, CH * HD), low),
            pltpu.VMEM((share, CH * HD), low),
            pltpu.VMEM((n, SUB, share), low),
            dma((2,)), dma((HK,)),
            dma((n,)), dma((n,)), dma((n,)), dma((n,)), dma((n,)), dma((n,)),
            dma((RG,)), dma((RG,)), dma((RG, CH)), dma((RG, CH)), dma((n,)), dma((n,)),
            dma((3,)), dma, dma, dma((RG,)), dma((RG,)),
        ],
        compiler_params=pltpu.CompilerParams(
            collective_id=0, has_side_effects=True, vmem_limit_bytes=56 * 1024 * 1024
        ),
    )(doc_lengths, block_plan, inverse_plan, queries[0], key_rows[0], value_rows[0], out_grad[0], kv_weight[0])
    return (query_grad[None], input_grad[None])


def solution(mesh):
    spec = P("section", "ctx", None)
    return jax.shard_map(
        shards, mesh=mesh, in_specs=(spec,) * 5 + (P(), P()), out_specs=(spec, spec), check_vma=False
    )
```

profile of v0, /device:TPU:69, one launch (start us, length us, event | category | flops | bytes accessed | tf_op | source)
XLA Modules:
  0.0 241.4 jit_solution(460892064624607714)
XLA Ops:
  0.6 1.3 select_reduce_fusion.inv
  1.9 235.7 %shard_map.86 = (bf16[128,4096]{1,0:T(8,128)(2,1)}, bf16[128,8192]{1,0:T(8,128)(2,1)}) custom-call(s32[16]{0:T(128)} %lens.1, s32[32]{0:T(128)} %plan.1, s32[32]{0:T(128)} %select_reduce_fusion.inv, bf16[128,4096]{1,0:T(8,128)(2,1)} %bitcast.8, bf16[128,512]{1,0:T(8,128)(2,1)} %bitcast.12, bf16[128,512]{1,0:T(8,128)(2,1)} %bitcast.13, ...), custom_call_target="tpu_custom_call" | custom-call | tf_op jit(solution)/shard_map/pallas_call | solution.py:335
  237.6 0.0 copy-start
  237.6 2.4 %copy.11 = bf16[1,128,4096]{2,1,0:T(8,128)(2,1)} copy(bf16[1,128,4096]{2,1,0:T(8,128)(2,1)} %bitcast.10) | data formatting | bytes 2097152
  240.0 0.0 copy-done
  240.0 1.3 copy.12
Async XLA Ops:
  237.6 2.4 %copy-start = (bf16[128,8192]{1,0:T(8,128)(2,1)S(1)}, bf16[128,8192]{1,0:T(8,128)(2,1)}, u32[]{:S(2)}) copy-start(bf16[128,8192]{1,0:T(8,128)(2,1)} %get-tuple-element.5) | copy-start | bytes 6291460
where the time goes:
time: 241 us
  Pallas kernels  236 us (98%)
  local copies, waits for them, and re-layouts  3.76 us (2%)
    pallas_call x1, Pallas kernels, shards(): pl.pallas_call(functools.partial(kernel, n, sections), out_shape=(jax.Sha...  236 us

commit v1 on v0

v1 whole, which is shorter than its diff:
```python
import functools
import math

import jax
import jax.numpy as jnp
from jax import lax
from jax.experimental import pallas as pl
from jax.experimental.pallas import tpu as pltpu
from jax.sharding import PartitionSpec as P

HQ = 32
HK = 4
HD = 128
BLOCK = 128
GROUP = HQ // HK
BACK = 8
SLOTS = BACK + 1
CH = 2 * HK
SUB = 32
RG = BLOCK // SUB
MASKED = -1e30
MIX = 13
KEYS = 384
MESH = pl.DeviceIdType.MESH


def rem(a, b):
    return lax.rem(a, b)


def div(a, b):
    return lax.div(a, b)


def kernel(
    n, sections, lens, plan, inv, q_hbm, k_ref, v_ref, o_hbm, w_hbm, dq_hbm, out_hbm,
    q_s, o_s, dq_s, kvw, recv1, send2, bias, s_s, g_s, part, recv3, kvo, kvg, wsh, wfull, outs,
    in_sem, dq_sem, s1s, s1r, s2s, s2r, s3s, s3r, xs, xr, gs, gr, os_, or_, loc_sem, wxs, wxr, wgs, wgr,
):
    me = lax.axis_index("ctx")
    sec = lax.axis_index("section")
    rg = div(me, CH)
    ch = rem(me, CH)
    core = rem(ch, 2)
    column = div(ch, 2)
    before = rem(sec + sections - 1, sections)

    def remote(src, dst, send, recv, **where):
        return pltpu.make_async_remote_copy(
            src_ref=src, dst_ref=dst, send_sem=send, recv_sem=recv,
            device_id=where, device_id_type=MESH,
        )

    def rows(group):
        return pl.ds(pl.multiple_of(group * SUB, SUB), SUB)

    def others(body):
        def step(k, carry):
            body(rem(me + MIX * k, n))
            return carry
        lax.fori_loop(1, n, step, 0)

    load_q = pltpu.make_async_copy(q_hbm, q_s, in_sem.at[0])
    load_o = pltpu.make_async_copy(o_hbm, o_s, in_sem.at[1])
    load_q.start()
    load_o.start()

    barrier = pltpu.get_barrier_semaphore()
    others(lambda j: pl.semaphore_signal(barrier, inc=1, device_id={"ctx": j}, device_id_type=MESH))
    pl.semaphore_signal(barrier, inc=1, device_id={"section": rem(sec + 1, sections)}, device_id_type=MESH)
    for head in range(HK):
        kvw[head, BACK] = k_ref[:, head * HD:(head + 1) * HD]
        kvw[HK + head, BACK] = v_ref[:, head * HD:(head + 1) * HD]
    pl.semaphore_wait(barrier, n)

    def piece_out(j):
        return remote(kvw.at[rem(j, CH), BACK, rows(div(j, CH))], recv1.at[me], s1s.at[j], s1r.at[me], ctx=j)

    others(lambda j: piece_out(j).start())
    w_shift = remote(w_hbm, wsh, wxs, wxr, section=before)
    w_shift.start()
    recv1[me] = kvw[ch, BACK, rows(rg)]

    token_block = plan[me]
    row_token = token_block * BLOCK + lax.broadcasted_iota(jnp.int32, (1, BLOCK), 1)
    start = jnp.zeros((1, BLOCK), jnp.int32)
    end = jnp.int32(0)
    for j in range(lens.shape[0]):
        end = end + lens[j]
        start = jnp.where(row_token >= end, end, start)
    key_token = (token_block - BACK) * BLOCK + lax.broadcasted_iota(jnp.int32, (SLOTS * BLOCK, BLOCK), 0)
    seen = jnp.logical_and(key_token >= start, key_token <= row_token)
    bias[...] = jnp.where(seen, 0.0, MASKED)

    def piece_in(j):
        return remote(kvw.at[0, BACK, rows(0)], recv1.at[j], s1s.at[j], s1r.at[j], ctx=j)

    others(lambda j: piece_in(j).wait_recv())

    def window_out(d):
        return remote(send2.at[d], kvw.at[ch, pl.ds(0, BACK), rows(rg)], s2s.at[d], s2r.at[me], ctx=d)

    head_of = rem(ch, HK)

    def window_own():
        return pltpu.make_async_copy(send2.at[me], kvw.at[ch, pl.ds(0, BACK), rows(rg)], loc_sem.at[0])

    def window_step(i, carry):
        d = HK * rem(div(me, HK) + 3 * i, n // HK) + rem(head_of - div(i, n // HK) + HK, HK)
        first = plan[d] - BACK
        for w in range(BACK):
            send2[d, w] = recv1[inv[jnp.maximum(first + w, 0)]]

        @pl.when(d != me)
        def _():
            window_out(d).start()

        @pl.when(d == me)
        def _():
            window_own().start()
        return carry

    lax.fori_loop(0, n, window_step, 0)

    def window_in(j):
        return remote(send2.at[j], kvw.at[rem(j, CH), pl.ds(0, BACK), rows(div(j, CH))], s2s.at[j], s2r.at[j], ctx=j)

    w_slot = rem(rg, 2) * 2 + core

    def w_rows(slot):
        return wfull.at[pl.ds(pl.multiple_of(slot * w_hbm.shape[0], 256), w_hbm.shape[0])]

    def w_target(z):
        return z * CH + 2 * column + div(rg, 2)

    def w_source(u):
        return (2 * core + u // 2) * CH + 2 * column + u % 2

    def w_out(z):
        return remote(wsh, w_rows(w_slot), wgs.at[z], wgr.at[w_slot], ctx=w_target(z))

    def w_own():
        return pltpu.make_async_copy(wsh, w_rows(w_slot), loc_sem.at[1])

    def spread_weights():
        w_shift.wait_recv()
        for z in range(RG):
            @pl.when(w_target(z) != me)
            def _():
                w_out(z).start()

            @pl.when(w_target(z) == me)
            def _():
                w_own().start()

    load_q.wait()
    load_o.wait()

    scale = 1.0 / math.sqrt(HD)
    power = scale * math.log2(math.e)
    nt = (((1,), (1,)), ((), ()))
    tn = (((0,), (0,)), ((), ()))

    def part_out(j):
        return remote(part.at[rem(j, CH), :, rows(div(j, CH))], recv3.at[me], s3s.at[j], s3r.at[me], ctx=j)

    def part_own():
        return pltpu.make_async_copy(part.at[ch, :, rows(rg)], recv3.at[me], loc_sem.at[2])

    def one_head(step, carry):
        head = rem(step + me, HK)

        def arrived(i, carry):
            j = HK * i + head

            @pl.when(j != me)
            def _():
                window_in(j).wait_recv()

            @pl.when(j == me)
            def _():
                window_own().wait()
            return carry

        lax.fori_loop(0, n // HK, arrived, 0)

        @pl.when(step == 1)
        def _():
            spread_weights()

        def columns(i):
            return pl.ds(pl.multiple_of((head * GROUP + i) * HD, HD), HD)

        q2 = jnp.concatenate([q_s[:, columns(i)] for i in range(GROUP)], axis=0)
        o2 = jnp.concatenate([o_s[:, columns(i)] for i in range(GROUP)], axis=0)
        wide = GROUP * BLOCK
        spans = [(slice(i, i + KEYS), slice(i // BLOCK, (i + KEYS) // BLOCK)) for i in range(0, SLOTS * BLOCK, KEYS)]

        def folded(x, over):
            return over(x.reshape(KEYS // 8, 8, wide), axis=0)

        peak = None
        for span, slots in spans:
            b = bias[span]
            keys = kvw[head, slots].reshape(KEYS, HD)
            scores = lax.dot_general(keys, q2, nt, preferred_element_type=jnp.float32)
            scores = scores + jnp.concatenate([b] * GROUP, axis=1)
            s_s[span] = scores
            top = folded(scores, jnp.max)
            peak = top if peak is None else jnp.maximum(peak, top)
            values = kvw[HK + head, slots].reshape(KEYS, HD)
            g_s[span] = lax.dot_general(values, o2, nt, preferred_element_type=jnp.float32)
        peak = jnp.max(peak, axis=0, keepdims=True)
        total = jnp.zeros((8, wide), jnp.float32)
        weighted = jnp.zeros((8, wide), jnp.float32)
        for span, slots in spans:
            terms = jnp.exp2((s_s[span] - peak) * power)
            s_s[span] = terms
            total = total + folded(terms, jnp.sum)
            weighted = weighted + folded(terms * g_s[span], jnp.sum)
        inverse = 1.0 / jnp.sum(total, axis=0, keepdims=True)
        delta = jnp.sum(weighted, axis=0, keepdims=True) * inverse
        dq = jnp.zeros((wide, HD), jnp.float32)
        for span, slots in spans:
            prob = s_s[span] * inverse
            prob_low = prob.astype(jnp.bfloat16)
            score_low = (prob * (g_s[span] - delta)).astype(jnp.bfloat16)
            dv = jnp.dot(prob_low, o2, preferred_element_type=jnp.float32)
            dk = jnp.dot(score_low, q2, preferred_element_type=jnp.float32) * scale
            part[HK + head, slots] = dv.astype(jnp.bfloat16).reshape(KEYS // BLOCK, BLOCK, HD)
            part[head, slots] = dk.astype(jnp.bfloat16).reshape(KEYS // BLOCK, BLOCK, HD)
            keys = kvw[head, slots].reshape(KEYS, HD)
            dq = dq + lax.dot_general(score_low, keys, tn, preferred_element_type=jnp.float32)
        for i in range(GROUP):
            dq_s[:, columns(i)] = (dq[i * BLOCK:(i + 1) * BLOCK] * scale).astype(jnp.bfloat16)

        def send(i, carry):
            turn = rem(3 * i + div(me, HK), n // HK)
            j = turn * HK + head

            @pl.when(j != me)
            def _():
                part_out(j).start()

            @pl.when(j == me)
            def _():
                part_own().start()
            return carry

        lax.fori_loop(0, 2 * RG, send, 0)
        wide = pl.ds(pl.multiple_of(head * GROUP * HD, GROUP * HD), GROUP * HD)
        pltpu.make_async_copy(dq_s.at[:, wide], dq_hbm.at[:, wide], dq_sem.at[head]).start()
        return carry

    lax.fori_loop(0, HK, one_head, 0)

    def part_in(j):
        return remote(part.at[0, :, rows(0)], recv3.at[j], s3s.at[j], s3r.at[j], ctx=j)

    others(lambda j: part_in(j).wait_recv())
    part_own().wait()

    per = n // RG

    def owner(chunk, i):
        z = div(i, 2)
        return z * CH + 2 * rem(chunk - z + RG, RG) + rem(i, 2)

    def blocks(chunk):
        return pl.ds(pl.multiple_of(chunk * per, per), per)

    def x_copy(chunk):
        return remote(kvo.at[blocks(chunk)], kvg.at[ch, blocks(chunk)], xs.at[chunk], xr.at[chunk], section=before)

    def reduce_chunk(step, carry):
        chunk = rem(step + rg, RG)

        def one_block(i, carry):
            p = owner(chunk, i)
            total = jnp.zeros((SUB, HD), jnp.float32)
            for w in range(SLOTS):
                later = plan[p] + BACK - w
                term = recv3[inv[jnp.minimum(later, n - 1)], w].astype(jnp.float32)
                total = total + jnp.where(later < n, term, 0.0)
            kvo[chunk * per + i] = total.astype(jnp.bfloat16)
            return carry

        lax.fori_loop(0, per, one_block, 0)
        x_copy(chunk).start()
        return carry

    lax.fori_loop(0, RG, reduce_chunk, 0)

    sibling = rg * CH + 2 * column + 1 - core

    def gather(chunk, source, target, slot):
        return remote(
            kvg.at[source, blocks(chunk)], kvg.at[source, blocks(chunk)],
            gs.at[chunk, slot], gr.at[chunk, source], ctx=target,
        )

    def along(i):
        return 2 * rem(column + i, RG)

    def gather_chunk(step, carry):
        chunk = rem(step + rg, RG)
        x_copy(chunk).wait_recv()
        for i in range(1, RG):
            gather(chunk, ch, rg * CH + along(i) + core, i).start()
        gather(chunk, ch, sibling, 0).start()
        return carry

    lax.fori_loop(0, RG, gather_chunk, 0)

    def share_chunk(step, carry):
        chunk = rem(step + rg, RG)
        for i in range(1, RG):
            source = along(i) + core
            gather(chunk, source, sibling, RG + i).wait_recv()
            gather(chunk, source, sibling, RG + i).start()
        return carry

    lax.fori_loop(0, RG, share_chunk, 0)

    for u in range(RG):
        @pl.when(w_source(u) != me)
        def _():
            remote(wsh, w_rows(u), wgs.at[u], wgr.at[u], ctx=w_source(u)).wait_recv()

        @pl.when(w_source(u) == me)
        def _():
            w_own().wait()

    wide = wfull.shape[0] // 2

    def out_part(j, v):
        first = (2 * rem(j, 2) + v) * CH * wide // 2 + rem(div(j, 2), RG) * wide
        return out_hbm.at[rows(div(j, CH)), pl.ds(pl.multiple_of(first, wide), wide)]

    def out_copy(index, p, v):
        return remote(outs.at[v, index], out_part(me, v), os_.at[v, p], or_.at[v, me], ctx=p)

    def out_own(index, v):
        return pltpu.make_async_copy(outs.at[v, index], out_part(me, v), loc_sem.at[3 + v])

    def multiply_chunk(step, carry):
        chunk = rem(step + rg, RG)
        for i in range(RG):
            source = along(i) + 1 - core
            gather(chunk, source, sibling, 0).wait_recv()
        left = jnp.concatenate([kvg[i, blocks(chunk)].reshape(per * SUB, HD) for i in range(CH)], axis=1)
        for v in range(2):
            product = lax.dot_general(left, wfull[v * wide:(v + 1) * wide], nt, preferred_element_type=jnp.float32)
            outs[v, blocks(chunk)] = product.astype(jnp.bfloat16).reshape(per, SUB, wide)

            def send(i, carry):
                turn = rem(3 * i + ch, per)
                p = owner(chunk, turn)

                @pl.when(p != me)
                def _():
                    out_copy(chunk * per + turn, p, v).start()

                @pl.when(p == me)
                def _():
                    out_own(chunk * per + turn, v).start()
                return carry

            lax.fori_loop(0, per, send, 0)
        return carry

    lax.fori_loop(0, RG, multiply_chunk, 0)

    others(lambda j: piece_out(j).wait_send())
    others(lambda j: window_out(j).wait_send())
    others(lambda j: part_out(j).wait_send())
    w_shift.wait_send()
    for z in range(RG):
        @pl.when(w_target(z) != me)
        def _():
            w_out(z).wait_send()

    def sent(chunk, carry):
        x_copy(chunk).wait_send()
        for i in range(1, RG):
            gather(chunk, ch, rg * CH + along(i) + core, i).wait_send()
            gather(chunk, ch, sibling, RG + i).wait_send()
        gather(chunk, ch, sibling, 0).wait_send()
        return carry

    lax.fori_loop(0, RG, sent, 0)
    for head in range(HK):
        wide_q = pl.ds(head * GROUP * HD, GROUP * HD)
        pltpu.make_async_copy(dq_s.at[:, wide_q], dq_hbm.at[:, wide_q], dq_sem.at[head]).wait()
    for v in range(2):
        others(lambda j: out_copy(0, j, v).wait_send())
        out_own(0, v).wait()
        others(lambda j: remote(outs.at[v, 0], out_part(j, v), os_.at[v, j], or_.at[v, j], ctx=j).wait_recv())


def shards(queries, key_rows, value_rows, out_grad, kv_weight, doc_lengths, block_plan):
    n = lax.axis_size("ctx")
    sections = lax.axis_size("section")
    number = jnp.arange(n, dtype=jnp.int32)
    inverse_plan = jnp.sum(jnp.where(block_plan[None, :] == number[:, None], number[None, :], 0), axis=1, dtype=jnp.int32)
    tokens, width = queries.shape[1:]
    features = kv_weight.shape[1]
    model = features * n
    share = model // CH
    per = n // RG
    smem = pl.BlockSpec(memory_space=pltpu.SMEM)
    vmem = pl.BlockSpec(memory_space=pltpu.VMEM)
    hbm = pl.BlockSpec(memory_space=pl.ANY)
    low = jnp.bfloat16
    dma = pltpu.SemaphoreType.DMA
    query_grad, input_grad = pl.pallas_call(
        functools.partial(kernel, n, sections),
        out_shape=(
            jax.ShapeDtypeStruct((tokens, width), low),
            jax.ShapeDtypeStruct((tokens, model), low),
        ),
        in_specs=[smem, smem, smem, hbm, vmem, vmem, hbm, hbm],
        out_specs=(hbm, hbm),
        scratch_shapes=[
            pltpu.VMEM((tokens, width), low),
            pltpu.VMEM((tokens, width), low),
            pltpu.VMEM((tokens, width), low),
            pltpu.VMEM((CH, SLOTS, BLOCK, HD), low),
            pltpu.VMEM((n, SUB, HD), low),
            pltpu.VMEM((n, BACK, SUB, HD), low),
            pltpu.VMEM((SLOTS * BLOCK, BLOCK), jnp.float32),
            pltpu.VMEM((SLOTS * BLOCK, GROUP * BLOCK), jnp.float32),
            pltpu.VMEM((SLOTS * BLOCK, GROUP * BLOCK), jnp.float32),
            pltpu.VMEM((CH, SLOTS, BLOCK, HD), low),
            pltpu.VMEM((n, SLOTS, SUB, HD), low),
            pltpu.VMEM((n, SUB, HD), low),
            pltpu.VMEM((CH, n, SUB, HD), low),
            pltpu.VMEM((features, CH * HD), low),
            pltpu.VMEM((share, CH * HD), low),
            pltpu.VMEM((2, n, SUB, share // 2), low),
            dma((2,)), dma((HK,)),
            dma((n,)), dma((n,)), dma((n,)), dma((n,)), dma((n,)), dma((n,)),
            dma((RG,)), dma((RG,)), dma((RG, CH)), dma((RG, CH)), dma((2, n)), dma((2, n)),
            dma((5,)), dma, dma, dma((RG,)), dma((RG,)),
        ],
        compiler_params=pltpu.CompilerParams(
            collective_id=0, has_side_effects=True, vmem_limit_bytes=56 * 1024 * 1024
        ),
    )(doc_lengths, block_plan, inverse_plan, queries[0], key_rows[0], value_rows[0], out_grad[0], kv_weight[0])
    return (query_grad[None], input_grad[None])


def solution(mesh):
    spec = P("section", "ctx", None)
    return jax.shard_map(
        shards, mesh=mesh, in_specs=(spec,) * 5 + (P(), P()), out_specs=(spec, spec), check_vma=False
    )
```

time: 241 us -> 147 us (0.61)
  the two profiles are of different devices: /device:TPU:69 before, /device:TPU:1 now
where the time goes in v1:
time: 147 us; the launch traced here: 145 us
  Pallas kernels  140 us (95%)
  local copies, waits for them, and re-layouts  3.76 us (3%)
    pallas_call x1, Pallas kernels, shards(): pl.pallas_call(functools.partial(kernel, n, sections), out_shape=(jax.Sha...  140 us
    unnamed x4, local copies, waits for them, and re-layouts  3.76 us

profile of v1, /device:TPU:1, one launch (start us, length us, event | category | flops | bytes accessed | tf_op | source)
XLA Modules:
  0.0 145.2 jit_solution(7945129376962406157)
XLA Ops:
  0.6 1.3 select_reduce_fusion.inv
  1.9 139.5 %shard_map.86 = (bf16[128,4096]{1,0:T(8,128)(2,1)}, bf16[128,8192]{1,0:T(8,128)(2,1)}) custom-call(s32[16]{0:T(128)} %lens.1, s32[32]{0:T(128)} %plan.1, s32[32]{0:T(128)} %select_reduce_fusion.inv, bf16[128,4096]{1,0:T(8,128)(2,1)} %bitcast.8, bf16[128,512]{1,0:T(8,128)(2,1)} %bitcast.12, bf16[128,512]{1,0:T(8,128)(2,1)} %bitcast.13, ...), custom_call_target="tpu_custom_call" | custom-call | tf_op jit(solution)/shard_map/pallas_call | solution.py:416
  141.5 0.0 copy-start
  141.5 2.4 %copy.11 = bf16[1,128,4096]{2,1,0:T(8,128)(2,1)} copy(bf16[1,128,4096]{2,1,0:T(8,128)(2,1)} %bitcast.10) | data formatting | bytes 2097152
  143.9 0.0 copy-done
  143.9 1.3 copy.12
Async XLA Ops:
  141.5 2.4 %copy-start = (bf16[128,8192]{1,0:T(8,128)(2,1)S(1)}, bf16[128,8192]{1,0:T(8,128)(2,1)}, u32[]{:S(2)}) copy-start(bf16[128,8192]{1,0:T(8,128)(2,1)} %get-tuple-element.5) | copy-start | bytes 6291460

commit v2 on v1

--- a/solution.py
+++ b/solution.py
@@ -20,6 +20,7 @@
 RG = BLOCK // SUB
 MASKED = -1e30
 MIX = 13
+HALVES = 2
 KEYS = 384
 MESH = pl.DeviceIdType.MESH
 
@@ -33,9 +34,9 @@
 
 
 def kernel(
-    n, sections, lens, plan, inv, q_hbm, k_ref, v_ref, o_hbm, w_hbm, dq_hbm, out_hbm,
-    q_s, o_s, dq_s, kvw, recv1, send2, bias, s_s, g_s, part, recv3, kvo, kvg, wsh, wfull, outs,
-    in_sem, dq_sem, s1s, s1r, s2s, s2r, s3s, s3r, xs, xr, gs, gr, os_, or_, loc_sem, wxs, wxr, wgs, wgr,
+    n, sections, lens, plan, q_hbm, k_ref, v_ref, o_hbm, w_hbm, dq_hbm, out_hbm,
+    inv, q_s, o_s, dq_s, kvw, recv1, send2, bias, s_s, g_s, part, recv3, kvo, xbuf, blk, wsh, wfull, outs,
+    in_sem, dq_sem, s1s, s1r, s2s, s2r, s3s, s3r, xs, xr, ds_, dr, gs, gr, os_, or_, own_sem, loc_sem, wxs, wxr, wgs, wgr,
 ):
     me = lax.axis_index("ctx")
     sec = lax.axis_index("section")
@@ -71,6 +72,15 @@
     for head in range(HK):
         kvw[head, BACK] = k_ref[:, head * HD:(head + 1) * HD]
         kvw[HK + head, BACK] = v_ref[:, head * HD:(head + 1) * HD]
+
+    def invert(b, carry):
+        place = jnp.int32(0)
+        for p in range(n):
+            place = jnp.where(plan[p] == b, p, place)
+        inv[b] = place
+        return carry
+
+    lax.fori_loop(0, n, invert, 0)
     pl.semaphore_wait(barrier, n)
 
     def piece_out(j):
@@ -125,19 +135,26 @@
     def window_in(j):
         return remote(send2.at[j], kvw.at[rem(j, CH), pl.ds(0, BACK), rows(div(j, CH))], s2s.at[j], s2r.at[j], ctx=j)
 
-    w_slot = rem(rg, 2) * 2 + core
+    place = rg * (1 - core) + column * core
+    w_slot = 2 * core + rem(place, 2)
+    shard = w_hbm.shape[0]
+
+    def device(z, y, core):
+        return z * CH + 2 * y + core
 
     def w_rows(slot):
-        return wfull.at[pl.ds(pl.multiple_of(slot * w_hbm.shape[0], 256), w_hbm.shape[0])]
-
-    def w_target(z):
-        return z * CH + 2 * column + div(rg, 2)
+        return wfull.at[pl.ds(pl.multiple_of(slot * shard, shard), shard)]
+
+    def w_target(i):
+        return device(i * (1 - core) + rg * core, column * (1 - core) + i * core, div(place, 2))
 
     def w_source(u):
-        return (2 * core + u // 2) * CH + 2 * column + u % 2
-
-    def w_out(z):
-        return remote(wsh, w_rows(w_slot), wgs.at[z], wgr.at[w_slot], ctx=w_target(z))
+        if u < 2:
+            return device(2 * core + u, column, 0)
+        return device(rg, 2 * core + u - 2, 1)
+
+    def w_out(i):
+        return remote(wsh, w_rows(w_slot), wgs.at[i], wgr.at[w_slot], ctx=w_target(i))
 
     def w_own():
         return pltpu.make_async_copy(wsh, w_rows(w_slot), loc_sem.at[1])
@@ -183,10 +200,6 @@
             return carry
 
         lax.fori_loop(0, n // HK, arrived, 0)
-
-        @pl.when(step == 1)
-        def _():
-            spread_weights()
 
         def columns(i):
             return pl.ds(pl.multiple_of((head * GROUP + i) * HD, HD), HD)
@@ -259,6 +272,7 @@
 
     others(lambda j: part_in(j).wait_recv())
     part_own().wait()
+    spread_weights()
 
     per = n // RG
 
@@ -270,7 +284,7 @@
         return pl.ds(pl.multiple_of(chunk * per, per), per)
 
     def x_copy(chunk):
-        return remote(kvo.at[blocks(chunk)], kvg.at[ch, blocks(chunk)], xs.at[chunk], xr.at[chunk], section=before)
+        return remote(kvo.at[blocks(chunk)], xbuf.at[blocks(chunk)], xs.at[chunk], xr.at[chunk], section=before)
 
     def reduce_chunk(step, carry):
         chunk = rem(step + rg, RG)
@@ -291,36 +305,75 @@
 
     lax.fori_loop(0, RG, reduce_chunk, 0)
 
-    sibling = rg * CH + 2 * column + 1 - core
-
-    def gather(chunk, source, target, slot):
-        return remote(
-            kvg.at[source, blocks(chunk)], kvg.at[source, blocks(chunk)],
-            gs.at[chunk, slot], gr.at[chunk, source], ctx=target,
-        )
-
-    def along(i):
-        return 2 * rem(column + i, RG)
-
-    def gather_chunk(step, carry):
+    def deliver(index, p):
+        return remote(xbuf.at[index], blk.at[0, 0, ch, rows(rg)], ds_.at[p], dr.at[me], ctx=p)
+
+    def deliver_own(index):
+        return pltpu.make_async_copy(xbuf.at[index], blk.at[0, 0, ch, rows(rg)], loc_sem.at[3])
+
+    def deliver_chunk(step, carry):
         chunk = rem(step + rg, RG)
         x_copy(chunk).wait_recv()
-        for i in range(1, RG):
-            gather(chunk, ch, rg * CH + along(i) + core, i).start()
-        gather(chunk, ch, sibling, 0).start()
+
+        def one(i, carry):
+            turn = rem(3 * i + ch, per)
+            p = owner(chunk, turn)
+
+            @pl.when(p != me)
+            def _():
+                deliver(chunk * per + turn, p).start()
+
+            @pl.when(p == me)
+            def _():
+                deliver_own(chunk * per + turn).start()
+            return carry
+
+        lax.fori_loop(0, per, one, 0)
         return carry
 
-    lax.fori_loop(0, RG, gather_chunk, 0)
-
-    def share_chunk(step, carry):
-        chunk = rem(step + rg, RG)
-        for i in range(1, RG):
-            source = along(i) + core
-            gather(chunk, source, sibling, RG + i).wait_recv()
-            gather(chunk, source, sibling, RG + i).start()
-        return carry
-
-    lax.fori_loop(0, RG, share_chunk, 0)
+    lax.fori_loop(0, RG, deliver_chunk, 0)
+
+    def delivered(j):
+        return remote(xbuf.at[0], blk.at[0, 0, rem(j, CH), rows(div(j, CH))], ds_.at[j], dr.at[j], ctx=j)
+
+    others(lambda j: delivered(j).wait_recv())
+    deliver_own(0).wait()
+
+    sibling = device(rg, column, 1 - core)
+    half = BLOCK // HALVES
+
+    def half_rows(q):
+        return pl.ds(pl.multiple_of(q * half, half), half)
+
+    def chip(axis, i, core):
+        return device(rem(rg + axis * i, RG), rem(column + (1 - axis) * i, RG), core)
+
+    def along(q, axis, i):
+        return remote(
+            blk.at[0, 0, :, half_rows(q)], blk.at[3 * axis + RG - i, 0, :, half_rows(q)],
+            gs.at[q, 3 * axis + i], gr.at[q, 3 * axis + RG - i, 0], ctx=chip(axis, i, core),
+        )
+
+    def across(q, spot):
+        return remote(
+            blk.at[spot, 0, :, half_rows(q)], blk.at[spot, 1, :, half_rows(q)],
+            gs.at[q, 7 + spot], gr.at[q, spot, 1], ctx=sibling,
+        )
+
+    def arrival(q, spot, other):
+        return remote(
+            blk.at[spot, other, :, half_rows(q)], blk.at[spot, other, :, half_rows(q)],
+            gs.at[q, 0], gr.at[q, spot, other], ctx=sibling,
+        )
+
+    def far(t):
+        return t + (t // 2) * (5 - 2 * t)
+
+    for q in range(HALVES):
+        for t in range(1, RG):
+            for axis in range(2):
+                along(q, axis, far(t)).start()
+        across(q, 0).start()
 
     for u in range(RG):
         @pl.when(w_source(u) != me)
@@ -331,45 +384,67 @@
         def _():
             w_own().wait()
 
-    wide = wfull.shape[0] // 2
-
-    def out_part(j, v):
-        first = (2 * rem(j, 2) + v) * CH * wide // 2 + rem(div(j, 2), RG) * wide
-        return out_hbm.at[rows(div(j, CH)), pl.ds(pl.multiple_of(first, wide), wide)]
-
-    def out_copy(index, p, v):
-        return remote(outs.at[v, index], out_part(me, v), os_.at[v, p], or_.at[v, me], ctx=p)
-
-    def out_own(index, v):
-        return pltpu.make_async_copy(outs.at[v, index], out_part(me, v), loc_sem.at[3 + v])
-
-    def multiply_chunk(step, carry):
-        chunk = rem(step + rg, RG)
-        for i in range(RG):
-            source = along(i) + 1 - core
-            gather(chunk, source, sibling, 0).wait_recv()
-        left = jnp.concatenate([kvg[i, blocks(chunk)].reshape(per * SUB, HD) for i in range(CH)], axis=1)
-        for v in range(2):
-            product = lax.dot_general(left, wfull[v * wide:(v + 1) * wide], nt, preferred_element_type=jnp.float32)
-            outs[v, blocks(chunk)] = product.astype(jnp.bfloat16).reshape(per, SUB, wide)
-
-            def send(i, carry):
-                turn = rem(3 * i + ch, per)
-                p = owner(chunk, turn)
-
-                @pl.when(p != me)
+    def out_part(j, axis, v, q):
+        z, y, b = div(j, CH), rem(div(j, 2), RG), rem(j, 2)
+        number = (1 - axis) * device(2 * b + v, y, 0) + axis * device(z, 2 * b + v, 1)
+        return out_hbm.at[half_rows(q), pl.ds(pl.multiple_of(number * shard, shard), shard)]
+
+    def out_copy(q, axis, i, other, v):
+        core_there = core + other * (1 - 2 * core)
+        return remote(
+            outs.at[q, axis, i, other, v], out_part(me, axis, v, q),
+            os_.at[q, axis, i, other, v], or_.at[q, axis, rem(RG - i, RG), other, v], ctx=chip(axis, i, core_there),
+        )
+
+    def out_own(q, axis, v):
+        return pltpu.make_async_copy(outs.at[q, axis, 0, 0, v], out_part(me, axis, v, q), own_sem.at[q, axis, v])
+
+    def multiply(q):
+        def one(m, carry):
+            axis, t = rem(m, 2), div(m, 2)
+            i = t + div(t, 2) * (5 - 2 * t)
+            spot = jnp.where(i == 0, 0, 3 * axis + i)
+
+            @pl.when(m != 1)
+            def _():
+                arrival(q, spot, 1).wait_recv()
+
+            left = jnp.concatenate(
+                [
+                    jnp.concatenate([blk[spot, other, c, q * half:(q + 1) * half] for c in range(CH)], axis=1)
+                    for other in range(2)
+                ],
+                axis=0,
+            )
+            right = wfull[pl.ds(pl.multiple_of(axis * 2 * shard, 2 * shard), 2 * shard)]
+            product = lax.dot_general(left, right, nt, preferred_element_type=jnp.float32).astype(jnp.bfloat16)
+            for other in range(2):
+                for v in range(2):
+                    outs[q, axis, i, other, v] = product[other * half:(other + 1) * half, v * shard:(v + 1) * shard]
+            for v in range(2):
+                out_copy(q, axis, i, 1, v).start()
+
+                @pl.when(i != 0)
                 def _():
-                    out_copy(chunk * per + turn, p, v).start()
-
-                @pl.when(p == me)
+                    out_copy(q, axis, i, 0, v).start()
+
+                @pl.when(i == 0)
                 def _():
-                    out_own(chunk * per + turn, v).start()
-                return carry
-
-            lax.fori_loop(0, per, send, 0)
-        return carry
-
-    lax.fori_loop(0, RG, multiply_chunk, 0)
+                    out_own(q, axis, v).start()
+            return carry
+
+        lax.fori_loop(0, 2 * RG, one, 0)
+
+    for q in range(HALVES):
+        def share(m, carry):
+            axis, t = rem(m, 2), div(m, 2)
+            spot = 3 * axis + t + div(t, 2) * (5 - 2 * t)
+            arrival(q, spot, 0).wait_recv()
+            across(q, spot).start()
+            return carry
+
+        lax.fori_loop(2, 2 * RG, share, 0)
+        multiply(q)
 
     others(lambda j: piece_out(j).wait_send())
     others(lambda j: window_out(j).wait_send())
@@ -380,34 +455,50 @@
         def _():
             w_out(z).wait_send()
 
-    def sent(chunk, carry):
-        x_copy(chunk).wait_send()
-        for i in range(1, RG):
-            gather(chunk, ch, rg * CH + along(i) + core, i).wait_send()
-            gather(chunk, ch, sibling, RG + i).wait_send()
-        gather(chunk, ch, sibling, 0).wait_send()
-        return carry
-
-    lax.fori_loop(0, RG, sent, 0)
+        x_copy(z).wait_send()
+
+    others(lambda j: deliver(0, j).wait_send())
+    for q in range(HALVES):
+        for axis in range(2):
+            for i in range(1, RG):
+                along(q, axis, i).wait_send()
+                across(q, 3 * axis + i).wait_send()
+        across(q, 0).wait_send()
     for head in range(HK):
         wide_q = pl.ds(head * GROUP * HD, GROUP * HD)
         pltpu.make_async_copy(dq_s.at[:, wide_q], dq_hbm.at[:, wide_q], dq_sem.at[head]).wait()
-    for v in range(2):
-        others(lambda j: out_copy(0, j, v).wait_send())
-        out_own(0, v).wait()
-        others(lambda j: remote(outs.at[v, 0], out_part(j, v), os_.at[v, j], or_.at[v, j], ctx=j).wait_recv())
+
+    def finish(m, carry):
+        axis, i = div(m, RG), rem(m, RG)
+        for q in range(HALVES):
+            for v in range(2):
+                for other in range(2):
+                    there = core + other * (1 - 2 * core)
+                    incoming = remote(
+                        outs.at[q, axis, i, other, v], out_part(chip(axis, i, there), axis, v, q),
+                        os_.at[q, axis, i, other, v], or_.at[q, axis, i, other, v], ctx=sibling,
+                    )
+
+                    @pl.when(i + other > 0)
+                    def _():
+                        out_copy(q, axis, i, other, v).wait_send()
+                        incoming.wait_recv()
+
+                @pl.when(i == 0)
+                def _():
+                    out_own(q, axis, v).wait()
+        return carry
+
+    lax.fori_loop(0, 2 * RG, finish, 0)
 
 
 def shards(queries, key_rows, value_rows, out_grad, kv_weight, doc_lengths, block_plan):
     n = lax.axis_size("ctx")
     sections = lax.axis_size("section")
-    number = jnp.arange(n, dtype=jnp.int32)
-    inverse_plan = jnp.sum(jnp.where(block_plan[None, :] == number[:, None], number[None, :], 0), axis=1, dtype=jnp.int32)
     tokens, width = queries.shape[1:]
     features = kv_weight.shape[1]
     model = features * n
     share = model // CH
-    per = n // RG
     smem = pl.BlockSpec(memory_space=pltpu.SMEM)
     vmem = pl.BlockSpec(memory_space=pltpu.VMEM)
     hbm = pl.BlockSpec(memory_space=pl.ANY)
@@ -419,9 +510,10 @@
             jax.ShapeDtypeStruct((tokens, width), low),
             jax.ShapeDtypeStruct((tokens, model), low),
         ),
-        in_specs=[smem, smem, smem, hbm, vmem, vmem, hbm, hbm],
+        in_specs=[smem, smem, hbm, vmem, vmem, hbm, hbm],
         out_specs=(hbm, hbm),
         scratch_shapes=[
+            pltpu.SMEM((n,), jnp.int32),
             pltpu.VMEM((tokens, width), low),
             pltpu.VMEM((tokens, width), low),
             pltpu.VMEM((tokens, width), low),
@@ -434,19 +526,21 @@
             pltpu.VMEM((CH, SLOTS, BLOCK, HD), low),
             pltpu.VMEM((n, SLOTS, SUB, HD), low),
             pltpu.VMEM((n, SUB, HD), low),
-            pltpu.VMEM((CH, n, SUB, HD), low),
+            pltpu.VMEM((n, SUB, HD), low),
+            pltpu.VMEM((7, 2, CH, BLOCK, HD), low),
             pltpu.VMEM((features, CH * HD), low),
             pltpu.VMEM((share, CH * HD), low),
-            pltpu.VMEM((2, n, SUB, share // 2), low),
+            pltpu.VMEM((HALVES, 2, RG, 2, 2, BLOCK // HALVES, features), low),
             dma((2,)), dma((HK,)),
             dma((n,)), dma((n,)), dma((n,)), dma((n,)), dma((n,)), dma((n,)),
-            dma((RG,)), dma((RG,)), dma((RG, CH)), dma((RG, CH)), dma((2, n)), dma((2, n)),
-            dma((5,)), dma, dma, dma((RG,)), dma((RG,)),
+            dma((RG,)), dma((RG,)), dma((n,)), dma((n,)), dma((HALVES, 14)), dma((HALVES, 7, 2)),
+            dma((HALVES, 2, RG, 2, 2)), dma((HALVES, 2, RG, 2, 2)), dma((HALVES, 2, 2)),
+            dma((4,)), dma, dma, dma((RG,)), dma((RG,)),
         ],
         compiler_params=pltpu.CompilerParams(
             collective_id=0, has_side_effects=True, vmem_limit_bytes=56 * 1024 * 1024
         ),
-    )(doc_lengths, block_plan, inverse_plan, queries[0], key_rows[0], value_rows[0], out_grad[0], kv_weight[0])
+    )(doc_lengths, block_plan, queries[0], key_rows[0], value_rows[0], out_grad[0], kv_weight[0])
     return (query_grad[None], input_grad[None])
 
 

time: 147 us -> 121 us (0.82)
  Pallas kernels: 140 us -> 116 us
    pallas_call x1, Pallas kernels: 140 us -> 116 us  [shards(): pl.pallas_call(functools.partial(kernel, n, sections), out_shape=(jax.Sha...]
where the time goes in v2:
time: 121 us
  Pallas kernels  116 us (96%)
  local copies, waits for them, and re-layouts  3.76 us (3%)
    pallas_call x1, Pallas kernels, shards(): pl.pallas_call(functools.partial(kernel, n, sections), out_shape=(jax.Sha...  116 us
    unnamed x4, local copies, waits for them, and re-layouts  3.76 us

profile of v2, /device:TPU:1, one launch (start us, length us, event | category | flops | bytes accessed | tf_op | source)
XLA Modules:
  0.0 120.5 jit_solution(5447748451201024967)
XLA Ops:
  0.6 116.1 %shard_map.86 = (bf16[128,4096]{1,0:T(8,128)(2,1)}, bf16[128,8192]{1,0:T(8,128)(2,1)}) custom-call(s32[16]{0:T(128)} %lens.1, s32[32]{0:T(128)} %plan.1, bf16[128,4096]{1,0:T(8,128)(2,1)} %bitcast.8, bf16[128,512]{1,0:T(8,128)(2,1)} %bitcast.12, bf16[128,512]{1,0:T(8,128)(2,1)} %bitcast.13, bf16[128,4096]{1,0:T(8,128)(2,1)} %bitcast.9, ...), custom_call_target="tpu_custom_call" | custom-call | tf_op jit(solution)/shard_map/pallas_call | solution.py:507
  116.8 0.0 copy-start
  116.8 2.4 %copy.11 = bf16[1,128,4096]{2,1,0:T(8,128)(2,1)} copy(bf16[1,128,4096]{2,1,0:T(8,128)(2,1)} %bitcast.10) | data formatting | bytes 2097152
  119.2 0.0 copy-done
  119.2 1.3 %copy.12 = bf16[1,128,8192]{2,1,0:T(8,128)(2,1)} copy(bf16[1,128,8192]{2,1,0:T(8,128)(2,1)S(1)} %bitcast.7) | data formatting | bytes 4194304
Async XLA Ops:
  116.8 2.4 %copy-start = (bf16[128,8192]{1,0:T(8,128)(2,1)S(1)}, bf16[128,8192]{1,0:T(8,128)(2,1)}, u32[]{:S(2)}) copy-start(bf16[128,8192]{1,0:T(8,128)(2,1)} %get-tuple-element.5) | copy-start | bytes 6291460

commit v3 on v2

--- a/solution.py
+++ b/solution.py
@@ -34,9 +34,9 @@
 
 
 def kernel(
-    n, sections, lens, plan, q_hbm, k_ref, v_ref, o_hbm, w_hbm, dq_hbm, out_hbm,
-    inv, q_s, o_s, dq_s, kvw, recv1, send2, bias, s_s, g_s, part, recv3, kvo, xbuf, blk, wsh, wfull, outs,
-    in_sem, dq_sem, s1s, s1r, s2s, s2r, s3s, s3r, xs, xr, ds_, dr, gs, gr, os_, or_, own_sem, loc_sem, wxs, wxr, wgs, wgr,
+    n, sections, lens_hbm, plan_hbm, q_hbm, k_hbm, v_hbm, o_hbm, w_hbm, dq_hbm, out_hbm,
+    lens, plan, inv, q_s, o_s, dq_s, kvw, hold, send2, bias, s_s, g_s, part, terms, sums, totals, kvo, xbuf, blk, wsh, wfull, outs,
+    in_sem, kv_sem, dq_sem, s1s, s1r, g1s, g1r, s2s, s2r, s3s, s3r, rs, rr, xs, xr, ds_, dr, gs, gr, os_, or_, own_sem, loc_sem, wxs, wxr, wgs, wgr,
 ):
     me = lax.axis_index("ctx")
     sec = lax.axis_index("section")
@@ -52,44 +52,86 @@
             device_id=where, device_id_type=MESH,
         )
 
-    def rows(group):
-        return pl.ds(pl.multiple_of(group * SUB, SUB), SUB)
-
-    def others(body):
-        def step(k, carry):
-            body(rem(me + MIX * k, n))
-            return carry
-        lax.fori_loop(1, n, step, 0)
-
+    load_lens = pltpu.make_async_copy(lens_hbm, lens, in_sem.at[2])
+    load_plan = pltpu.make_async_copy(plan_hbm, plan, in_sem.at[3])
     load_q = pltpu.make_async_copy(q_hbm, q_s, in_sem.at[0])
     load_o = pltpu.make_async_copy(o_hbm, o_s, in_sem.at[1])
-    load_q.start()
-    load_o.start()
+    load_kv = [
+        pltpu.make_async_copy(
+            (v_hbm if kind else k_hbm).at[:, pl.ds(head * HD, HD)], kvw.at[kind * HK + head, BACK], kv_sem.at[kind, head]
+        )
+        for kind in range(2)
+        for head in range(HK)
+    ]
+    for load in (load_plan, load_lens, *load_kv, load_q, load_o):
+        load.start()
+
+    def device(z, y, core):
+        return z * CH + 2 * y + core
+
+    halves = BLOCK // 2
+    line = (2 * column + core, 2 * rg + core)
+
+    def mate(kind, m):
+        return device(rg, div(m, 2), rem(m, 2)) if kind == 0 else device(div(m, 2), column, rem(m, 2))
 
     barrier = pltpu.get_barrier_semaphore()
-    others(lambda j: pl.semaphore_signal(barrier, inc=1, device_id={"ctx": j}, device_id_type=MESH))
+
+    def greet(j):
+        pl.semaphore_signal(barrier, inc=1, device_id={"ctx": j}, device_id_type=MESH)
+
+    for k in range(1, CH):
+        greet(mate(0, rem(line[0] + k, CH)))
+    for k in range(1, RG):
+        for there in range(2):
+            greet(device(rem(rg + k, RG), column, there))
     pl.semaphore_signal(barrier, inc=1, device_id={"section": rem(sec + 1, sections)}, device_id_type=MESH)
-    for head in range(HK):
-        kvw[head, BACK] = k_ref[:, head * HD:(head + 1) * HD]
-        kvw[HK + head, BACK] = v_ref[:, head * HD:(head + 1) * HD]
+    load_plan.wait()
+    load_lens.wait()
 
     def invert(b, carry):
         place = jnp.int32(0)
         for p in range(n):
             place = jnp.where(plan[p] == b, p, place)
-        inv[b] = place
+        inv[0, b] = place
+        inv[1, b] = rem(div(place, 2), RG) * CH + div(place, CH) * 2 + rem(place, 2)
         return carry
 
     lax.fori_loop(0, n, invert, 0)
-    pl.semaphore_wait(barrier, n)
-
-    def piece_out(j):
-        return remote(kvw.at[rem(j, CH), BACK, rows(div(j, CH))], recv1.at[me], s1s.at[j], s1r.at[me], ctx=j)
-
-    others(lambda j: piece_out(j).start())
+    for load in load_kv:
+        load.wait()
+    pl.semaphore_wait(barrier, CH - 1 + 2 * (RG - 1) + 1)
+
+    def held_head(m):
+        return rem(div(m, 2) + 2 * rem(m, 2), HK)
+
+    def half_of(m):
+        return pl.ds(pl.multiple_of(rem(m, 2) * halves, halves), halves)
+
+    held = (me, column * CH + 2 * rg + core)
+
+    def piece_out(kind, m):
+        return remote(
+            kvw.at[kind * HK + held_head(m), BACK, half_of(m)], hold.at[kind, held[kind]],
+            s1s.at[kind, m], s1r.at[kind, line[kind]], ctx=mate(kind, m),
+        )
+
+    def piece_in(kind, m):
+        return remote(
+            kvw.at[0, BACK, half_of(0)], hold.at[kind, m if kind else rg * CH + m],
+            s1s.at[kind, m], s1r.at[kind, m], ctx=mate(kind, m),
+        )
+
+    def mates(body):
+        for k in range(1, CH):
+            for kind in range(2):
+                body(kind, rem(line[kind] + 3 * k, CH))
+
+    mates(lambda kind, m: piece_out(kind, m).start())
     w_shift = remote(w_hbm, wsh, wxs, wxr, section=before)
     w_shift.start()
-    recv1[me] = kvw[ch, BACK, rows(rg)]
+    for kind in range(2):
+        hold[kind, held[kind]] = kvw[kind * HK + held_head(line[kind]), BACK, half_of(line[kind])]
 
     token_block = plan[me]
     row_token = token_block * BLOCK + lax.broadcasted_iota(jnp.int32, (1, BLOCK), 1)
@@ -101,46 +143,68 @@
     key_token = (token_block - BACK) * BLOCK + lax.broadcasted_iota(jnp.int32, (SLOTS * BLOCK, BLOCK), 0)
     seen = jnp.logical_and(key_token >= start, key_token <= row_token)
     bias[...] = jnp.where(seen, 0.0, MASKED)
-
-    def piece_in(j):
-        return remote(kvw.at[0, BACK, rows(0)], recv1.at[j], s1s.at[j], s1r.at[j], ctx=j)
-
-    others(lambda j: piece_in(j).wait_recv())
-
-    def window_out(d):
-        return remote(send2.at[d], kvw.at[ch, pl.ds(0, BACK), rows(rg)], s2s.at[d], s2r.at[me], ctx=d)
-
-    head_of = rem(ch, HK)
-
-    def window_own():
-        return pltpu.make_async_copy(send2.at[me], kvw.at[ch, pl.ds(0, BACK), rows(rg)], loc_sem.at[0])
+    for kind in range(2):
+        terms[kind, CH] = jnp.zeros((SLOTS, halves, HD), jnp.bfloat16)
+
+    def group(kind, i):
+        across_lines = rg if kind == 0 else column
+        return hold.at[kind, pl.ds(pl.multiple_of(rem(across_lines + i, RG) * CH, CH), CH)]
+
+    def peer(kind, i):
+        return device(rem(rg + i, RG), column, core) if kind == 0 else device(rg, rem(column + i, RG), core)
+
+    def group_out(kind, i):
+        return remote(group(kind, 0), group(kind, 0), g1s.at[kind, i], g1r.at[kind, RG - i], ctx=peer(kind, i))
+
+    def group_in(kind, i):
+        return remote(group(kind, i), group(kind, i), g1s.at[kind, i], g1r.at[kind, i], ctx=peer(kind, i))
+
+    mates(lambda kind, m: piece_in(kind, m).wait_recv())
+    for i in (1, 3, 2):
+        for kind in range(2):
+            group_out(kind, i).start()
+    for i in (1, 3, 2):
+        for kind in range(2):
+            group_in(kind, i).wait_recv()
+
+    def window_slots(kind, m):
+        return kvw.at[kind * HK + held_head(m), pl.ds(0, BACK), half_of(m)]
+
+    def window_out(kind, m):
+        return remote(
+            send2.at[kind, m], window_slots(kind, line[kind]), s2s.at[kind, m], s2r.at[kind, line[kind]], ctx=mate(kind, m)
+        )
+
+    def window_own(kind):
+        return pltpu.make_async_copy(send2.at[kind, line[kind]], window_slots(kind, line[kind]), loc_sem.at[4 * kind])
+
+    def window_in(kind, m):
+        return remote(send2.at[kind, m], window_slots(kind, m), s2s.at[kind, m], s2r.at[kind, m], ctx=mate(kind, m))
+
+    turn_of = rem(rg + column, HK)
 
     def window_step(i, carry):
-        d = HK * rem(div(me, HK) + 3 * i, n // HK) + rem(head_of - div(i, n // HK) + HK, HK)
-        first = plan[d] - BACK
-        for w in range(BACK):
-            send2[d, w] = recv1[inv[jnp.maximum(first + w, 0)]]
-
-        @pl.when(d != me)
-        def _():
-            window_out(d).start()
-
-        @pl.when(d == me)
-        def _():
-            window_own().start()
+        for kind in range(2):
+            start_at = held_head(line[kind]) + 2 * RG - div(i, 2) - (rg if kind == 0 else column)
+            m = 2 * rem(start_at, RG) + rem(i, 2)
+            first = plan[mate(kind, m)] - BACK
+            for w in range(BACK):
+                send2[kind, m, w] = hold[kind, inv[kind, jnp.maximum(first + w, 0)]]
+
+            @pl.when(m != line[kind])
+            def _():
+                window_out(kind, m).start()
+
+            @pl.when(m == line[kind])
+            def _():
+                window_own(kind).start()
         return carry
 
-    lax.fori_loop(0, n, window_step, 0)
-
-    def window_in(j):
-        return remote(send2.at[j], kvw.at[rem(j, CH), pl.ds(0, BACK), rows(div(j, CH))], s2s.at[j], s2r.at[j], ctx=j)
+    lax.fori_loop(0, CH, window_step, 0)
 
     place = rg * (1 - core) + column * core
     w_slot = 2 * core + rem(place, 2)
     shard = w_hbm.shape[0]
-
-    def device(z, y, core):
-        return z * CH + 2 * y + core
 
     def w_rows(slot):
         return wfull.at[pl.ds(pl.multiple_of(slot * shard, shard), shard)]
@@ -178,28 +242,37 @@
     nt = (((1,), (1,)), ((), ()))
     tn = (((0,), (0,)), ((), ()))
 
-    def part_out(j):
-        return remote(part.at[rem(j, CH), :, rows(div(j, CH))], recv3.at[me], s3s.at[j], s3r.at[me], ctx=j)
-
-    def part_own():
-        return pltpu.make_async_copy(part.at[ch, :, rows(rg)], recv3.at[me], loc_sem.at[2])
+    def term_out(kind, m):
+        return remote(
+            part.at[kind * HK + held_head(m), :, half_of(m)], terms.at[kind, line[kind]],
+            s3s.at[kind, m], s3r.at[kind, line[kind]], ctx=mate(kind, m),
+        )
+
+    def term_own(kind):
+        m = line[kind]
+        return pltpu.make_async_copy(part.at[kind * HK + held_head(m), :, half_of(m)], terms.at[kind, m], loc_sem.at[2 + 3 * kind])
+
+    def term_in(kind, m):
+        return remote(
+            part.at[0, :, half_of(0)], terms.at[kind, m], s3s.at[kind, m], s3r.at[kind, m], ctx=mate(kind, m)
+        )
 
     def one_head(step, carry):
-        head = rem(step + me, HK)
-
-        def arrived(i, carry):
-            j = HK * i + head
-
-            @pl.when(j != me)
-            def _():
-                window_in(j).wait_recv()
-
-            @pl.when(j == me)
-            def _():
-                window_own().wait()
-            return carry
-
-        lax.fori_loop(0, n // HK, arrived, 0)
+        head = rem(step + turn_of, HK)
+        for half in range(2):
+            m = 2 * rem(head + RG - 2 * half, RG) + half
+            for kind in range(2):
+                @pl.when(m != line[kind])
+                def _():
+                    window_in(kind, m).wait_recv()
+
+                @pl.when(m == line[kind])
+                def _():
+                    window_own(kind).wait()
+
+        @pl.when(step == 1)
+        def _():
+            spread_weights()
 
         def columns(i):
             return pl.ds(pl.multiple_of((head * GROUP + i) * HD, HD), HD)
@@ -247,97 +320,100 @@
         for i in range(GROUP):
             dq_s[:, columns(i)] = (dq[i * BLOCK:(i + 1) * BLOCK] * scale).astype(jnp.bfloat16)
 
-        def send(i, carry):
-            turn = rem(3 * i + div(me, HK), n // HK)
-            j = turn * HK + head
-
-            @pl.when(j != me)
-            def _():
-                part_out(j).start()
-
-            @pl.when(j == me)
-            def _():
-                part_own().start()
-            return carry
-
-        lax.fori_loop(0, 2 * RG, send, 0)
+        for half in range(2):
+            m = 2 * rem(head + RG - 2 * half, RG) + half
+            for kind in range(2):
+                @pl.when(m != line[kind])
+                def _():
+                    term_out(kind, m).start()
+
+                @pl.when(m == line[kind])
+                def _():
+                    term_own(kind).start()
+
         wide = pl.ds(pl.multiple_of(head * GROUP * HD, GROUP * HD), GROUP * HD)
         pltpu.make_async_copy(dq_s.at[:, wide], dq_hbm.at[:, wide], dq_sem.at[head]).start()
         return carry
 
     lax.fori_loop(0, HK, one_head, 0)
 
-    def part_in(j):
-        return remote(part.at[0, :, rows(0)], recv3.at[j], s3s.at[j], s3r.at[j], ctx=j)
-
-    others(lambda j: part_in(j).wait_recv())
-    part_own().wait()
-    spread_weights()
-
-    per = n // RG
-
-    def owner(chunk, i):
-        z = div(i, 2)
-        return z * CH + 2 * rem(chunk - z + RG, RG) + rem(i, 2)
-
-    def blocks(chunk):
-        return pl.ds(pl.multiple_of(chunk * per, per), per)
-
-    def x_copy(chunk):
-        return remote(kvo.at[blocks(chunk)], xbuf.at[blocks(chunk)], xs.at[chunk], xr.at[chunk], section=before)
-
-    def reduce_chunk(step, carry):
-        chunk = rem(step + rg, RG)
-
-        def one_block(i, carry):
-            p = owner(chunk, i)
-            total = jnp.zeros((SUB, HD), jnp.float32)
-            for w in range(SLOTS):
-                later = plan[p] + BACK - w
-                term = recv3[inv[jnp.minimum(later, n - 1)], w].astype(jnp.float32)
-                total = total + jnp.where(later < n, term, 0.0)
-            kvo[chunk * per + i] = total.astype(jnp.bfloat16)
+    mates(lambda kind, m: term_in(kind, m).wait_recv())
+    for kind in range(2):
+        term_own(kind).wait()
+
+    def total_out(kind, i):
+        to = rem((rg if kind == 0 else column) + i, RG)
+        return remote(
+            sums.at[kind, pl.ds(pl.multiple_of(to * CH, CH), CH)], totals.at[kind, RG - i],
+            rs.at[kind, i], rr.at[kind, RG - i], ctx=peer(kind, i),
+        )
+
+    def total_in(kind, i):
+        return remote(
+            sums.at[kind, pl.ds(0, CH)], totals.at[kind, i], rs.at[kind, i], rr.at[kind, i], ctx=peer(kind, i)
+        )
+
+    for i in (1, 2, 3, 0):
+        for kind in range(2):
+            here = rg if kind == 0 else column
+            to = rem(here + i, RG)
+
+            def one_block(e, carry):
+                p = device(to, div(e, 2), rem(e, 2)) if kind == 0 else device(div(e, 2), to, rem(e, 2))
+                total = jnp.zeros((halves, HD), jnp.float32)
+                for w in range(SLOTS):
+                    later = plan[p] + BACK - w
+                    source = inv[kind, jnp.minimum(later, n - 1)]
+                    wanted = jnp.logical_and(later < n, div(source, CH) == here)
+                    total = total + terms[kind, jnp.where(wanted, rem(source, CH), CH), w].astype(jnp.float32)
+                sums[kind, to * CH + e] = total.astype(jnp.bfloat16)
+                return carry
+
+            lax.fori_loop(0, CH, one_block, 0)
+            if i > 0:
+                total_out(kind, i).start()
+
+    def x_copy(kind):
+        return remote(kvo.at[kind], xbuf.at[kind], xs.at[kind], xr.at[kind], section=before)
+
+    for kind in range(2):
+        here = rg if kind == 0 else column
+        for i in range(1, RG):
+            total_in(kind, i).wait_recv()
+
+        def one_sum(e, carry):
+            total = sums[kind, here * CH + e].astype(jnp.float32)
+            for i in range(1, RG):
+                total = total + totals[kind, i, e].astype(jnp.float32)
+            kvo[kind, e] = total.astype(jnp.bfloat16)
             return carry
 
-        lax.fori_loop(0, per, one_block, 0)
-        x_copy(chunk).start()
-        return carry
-
-    lax.fori_loop(0, RG, reduce_chunk, 0)
-
-    def deliver(index, p):
-        return remote(xbuf.at[index], blk.at[0, 0, ch, rows(rg)], ds_.at[p], dr.at[me], ctx=p)
-
-    def deliver_own(index):
-        return pltpu.make_async_copy(xbuf.at[index], blk.at[0, 0, ch, rows(rg)], loc_sem.at[3])
-
-    def deliver_chunk(step, carry):
-        chunk = rem(step + rg, RG)
-        x_copy(chunk).wait_recv()
-
-        def one(i, carry):
-            turn = rem(3 * i + ch, per)
-            p = owner(chunk, turn)
-
-            @pl.when(p != me)
-            def _():
-                deliver(chunk * per + turn, p).start()
-
-            @pl.when(p == me)
-            def _():
-                deliver_own(chunk * per + turn).start()
-            return carry
-
-        lax.fori_loop(0, per, one, 0)
-        return carry
-
-    lax.fori_loop(0, RG, deliver_chunk, 0)
-
-    def delivered(j):
-        return remote(xbuf.at[0], blk.at[0, 0, rem(j, CH), rows(div(j, CH))], ds_.at[j], dr.at[j], ctx=j)
-
-    others(lambda j: delivered(j).wait_recv())
-    deliver_own(0).wait()
+        lax.fori_loop(0, CH, one_sum, 0)
+        x_copy(kind).start()
+
+    def owned(kind, m):
+        return blk.at[0, 0, kind * HK + held_head(m), half_of(m)]
+
+    def deliver(kind, m):
+        return remote(
+            xbuf.at[kind, m], owned(kind, line[kind]), ds_.at[kind, m], dr.at[kind, line[kind]], ctx=mate(kind, m)
+        )
+
+    def deliver_own(kind):
+        return pltpu.make_async_copy(xbuf.at[kind, line[kind]], owned(kind, line[kind]), loc_sem.at[3 + 3 * kind])
+
+    def delivered(kind, m):
+        return remote(xbuf.at[kind, m], owned(kind, m), ds_.at[kind, m], dr.at[kind, m], ctx=mate(kind, m))
+
+    for kind in range(2):
+        x_copy(kind).wait_recv()
+        for k in range(1, CH):
+            deliver(kind, rem(line[kind] + 3 * k, CH)).start()
+        deliver_own(kind).start()
+
+    mates(lambda kind, m: delivered(kind, m).wait_recv())
+    for kind in range(2):
+        deliver_own(kind).wait()
 
     sibling = device(rg, column, 1 - core)
     half = BLOCK // HALVES
@@ -366,13 +442,19 @@
             gs.at[q, 0], gr.at[q, spot, other], ctx=sibling,
         )
 
-    def far(t):
-        return t + (t // 2) * (5 - 2 * t)
+    ways = ((1, 3), (3, 1))
+
+    def onward(q, axis):
+        to, source = ways[q]
+        return remote(
+            blk.at[3 * axis + source, 0, :, half_rows(q)], blk.at[3 * axis + 2, 0, :, half_rows(q)],
+            gs.at[q, 3 * axis + 2], gr.at[q, 3 * axis + 2, 0], ctx=chip(axis, to, core),
+        )
 
     for q in range(HALVES):
-        for t in range(1, RG):
+        for k in range(2):
             for axis in range(2):
-                along(q, axis, far(t)).start()
+                along(q, axis, ways[q][k]).start()
         across(q, 0).start()
 
     for u in range(RG):
@@ -399,7 +481,7 @@
     def out_own(q, axis, v):
         return pltpu.make_async_copy(outs.at[q, axis, 0, 0, v], out_part(me, axis, v, q), own_sem.at[q, axis, v])
 
-    def multiply(q):
+    def multiply(q, first, last):
         def one(m, carry):
             axis, t = rem(m, 2), div(m, 2)
             i = t + div(t, 2) * (5 - 2 * t)
@@ -433,35 +515,50 @@
                     out_own(q, axis, v).start()
             return carry
 
-        lax.fori_loop(0, 2 * RG, one, 0)
-
-    for q in range(HALVES):
-        def share(m, carry):
-            axis, t = rem(m, 2), div(m, 2)
-            spot = 3 * axis + t + div(t, 2) * (5 - 2 * t)
-            arrival(q, spot, 0).wait_recv()
-            across(q, spot).start()
-            return carry
-
-        lax.fori_loop(2, 2 * RG, share, 0)
-        multiply(q)
-
-    others(lambda j: piece_out(j).wait_send())
-    others(lambda j: window_out(j).wait_send())
-    others(lambda j: part_out(j).wait_send())
+        lax.fori_loop(first, last, one, 0)
+
+    def share(q, spots):
+        for k in spots:
+            for axis in range(2):
+                spot = 3 * axis + (2 if k == 2 else ways[q][1 - k])
+                arrival(q, spot, 0).wait_recv()
+                if k == 0:
+                    onward(q, axis).start()
+                across(q, spot).start()
+
+    near = 2 * RG - 2
+    share(0, (0, 1))
+    share(1, (0, 1))
+    multiply(0, 0, near)
+    share(0, (2,))
+    multiply(1, 0, near)
+    multiply(0, near, 2 * RG)
+    share(1, (2,))
+    multiply(1, near, 2 * RG)
+
+    mates(lambda kind, m: piece_out(kind, m).wait_send())
+    mates(lambda kind, m: window_out(kind, m).wait_send())
+    for i in range(1, RG):
+        for kind in range(2):
+            group_out(kind, i).wait_send()
+    mates(lambda kind, m: term_out(kind, m).wait_send())
+    mates(lambda kind, m: deliver(kind, m).wait_send())
+    for kind in range(2):
+        x_copy(kind).wait_send()
+        for i in range(1, RG):
+            total_out(kind, i).wait_send()
     w_shift.wait_send()
     for z in range(RG):
         @pl.when(w_target(z) != me)
         def _():
             w_out(z).wait_send()
 
-        x_copy(z).wait_send()
-
-    others(lambda j: deliver(0, j).wait_send())
     for q in range(HALVES):
         for axis in range(2):
+            along(q, axis, 1).wait_send()
+            along(q, axis, 3).wait_send()
+            onward(q, axis).wait_send()
             for i in range(1, RG):
-                along(q, axis, i).wait_send()
                 across(q, 3 * axis + i).wait_send()
         across(q, 0).wait_send()
     for head in range(HK):
@@ -499,9 +596,8 @@
     features = kv_weight.shape[1]
     model = features * n
     share = model // CH
-    smem = pl.BlockSpec(memory_space=pltpu.SMEM)
-    vmem = pl.BlockSpec(memory_space=pltpu.VMEM)
-    hbm = pl.BlockSpec(memory_space=pl.ANY)
+    hbm = pl.BlockSpec(memory_space=pltpu.HBM)
+    anywhere = pl.BlockSpec(memory_space=pl.ANY)
     low = jnp.bfloat16
     dma = pltpu.SemaphoreType.DMA
     query_grad, input_grad = pl.pallas_call(
@@ -510,32 +606,37 @@
             jax.ShapeDtypeStruct((tokens, width), low),
             jax.ShapeDtypeStruct((tokens, model), low),
         ),
-        in_specs=[smem, smem, hbm, vmem, vmem, hbm, hbm],
-        out_specs=(hbm, hbm),
+        in_specs=[hbm] * 7,
+        out_specs=(anywhere, anywhere),
         scratch_shapes=[
+            pltpu.SMEM(doc_lengths.shape, jnp.int32),
             pltpu.SMEM((n,), jnp.int32),
+            pltpu.SMEM((2, n), jnp.int32),
             pltpu.VMEM((tokens, width), low),
             pltpu.VMEM((tokens, width), low),
             pltpu.VMEM((tokens, width), low),
             pltpu.VMEM((CH, SLOTS, BLOCK, HD), low),
-            pltpu.VMEM((n, SUB, HD), low),
-            pltpu.VMEM((n, BACK, SUB, HD), low),
+            pltpu.VMEM((2, n, BLOCK // 2, HD), low),
+            pltpu.VMEM((2, CH, BACK, BLOCK // 2, HD), low),
             pltpu.VMEM((SLOTS * BLOCK, BLOCK), jnp.float32),
             pltpu.VMEM((SLOTS * BLOCK, GROUP * BLOCK), jnp.float32),
             pltpu.VMEM((SLOTS * BLOCK, GROUP * BLOCK), jnp.float32),
             pltpu.VMEM((CH, SLOTS, BLOCK, HD), low),
-            pltpu.VMEM((n, SLOTS, SUB, HD), low),
-            pltpu.VMEM((n, SUB, HD), low),
-            pltpu.VMEM((n, SUB, HD), low),
+            pltpu.VMEM((2, CH + 1, SLOTS, BLOCK // 2, HD), low),
+            pltpu.VMEM((2, n, BLOCK // 2, HD), low),
+            pltpu.VMEM((2, RG, CH, BLOCK // 2, HD), low),
+            pltpu.VMEM((2, CH, BLOCK // 2, HD), low),
+            pltpu.VMEM((2, CH, BLOCK // 2, HD), low),
             pltpu.VMEM((7, 2, CH, BLOCK, HD), low),
             pltpu.VMEM((features, CH * HD), low),
             pltpu.VMEM((share, CH * HD), low),
             pltpu.VMEM((HALVES, 2, RG, 2, 2, BLOCK // HALVES, features), low),
-            dma((2,)), dma((HK,)),
-            dma((n,)), dma((n,)), dma((n,)), dma((n,)), dma((n,)), dma((n,)),
-            dma((RG,)), dma((RG,)), dma((n,)), dma((n,)), dma((HALVES, 14)), dma((HALVES, 7, 2)),
+            dma((4,)), dma((2, HK)), dma((HK,)),
+            dma((2, CH)), dma((2, CH)), dma((2, RG)), dma((2, RG)), dma((2, CH)), dma((2, CH)), dma((2, CH)), dma((2, CH)),
+            dma((2, RG)), dma((2, RG)), dma((2,)), dma((2,)), dma((2, CH)), dma((2, CH)),
+            dma((HALVES, 14)), dma((HALVES, 7, 2)),
             dma((HALVES, 2, RG, 2, 2)), dma((HALVES, 2, RG, 2, 2)), dma((HALVES, 2, 2)),
-            dma((4,)), dma, dma, dma((RG,)), dma((RG,)),
+            dma((7,)), dma, dma, dma((RG,)), dma((RG,)),
         ],
         compiler_params=pltpu.CompilerParams(
             collective_id=0, has_side_effects=True, vmem_limit_bytes=56 * 1024 * 1024

time: 121 us -> 112 us (0.926)
  Pallas kernels: 116 us -> 107 us
    pallas_call x1, Pallas kernels: 116 us -> 107 us  [shards(): pl.pallas_call(functools.partial(kernel, n, sections), out_shape=(jax.Sha...]
where the time goes in v3:
time: 112 us
  Pallas kernels  107 us (96%)
  local copies, waits for them, and re-layouts  3.76 us (3%)
    pallas_call x1, Pallas kernels, shards(): pl.pallas_call(functools.partial(kernel, n, sections), out_shape=(jax.Sha...  107 us
    unnamed x4, local copies, waits for them, and re-layouts  3.76 us

profile of v3, /device:TPU:1, one launch (start us, length us, event | category | flops | bytes accessed | tf_op | source)
XLA Modules:
  0.0 111.8 jit_solution(1289610049053362228)
XLA Ops:
  0.6 107.4 %shard_map.86 = (bf16[128,4096]{1,0:T(8,128)(2,1)}, bf16[128,8192]{1,0:T(8,128)(2,1)}) custom-call(s32[16]{0:T(128)} %lens_hbm.1, s32[32]{0:T(128)} %plan_hbm.1, bf16[128,4096]{1,0:T(8,128)(2,1)} %bitcast.8, bf16[128,512]{1,0:T(8,128)(2,1)} %bitcast.12, bf16[128,512]{1,0:T(8,128)(2,1)} %bitcast.13, bf16[128,4096]{1,0:T(8,128)(2,1)} %bitcast.9, ...), custom_call_target="tpu_custom_call" | custom-call | tf_op jit(solution)/shard_map/pallas_call | solution.py:603
  108.0 0.0 copy-start
  108.1 2.4 %copy.11 = bf16[1,128,4096]{2,1,0:T(8,128)(2,1)} copy(bf16[1,128,4096]{2,1,0:T(8,128)(2,1)} %bitcast.10) | data formatting | bytes 2097152
  110.5 0.0 copy-done
  110.5 1.3 %copy.12 = bf16[1,128,8192]{2,1,0:T(8,128)(2,1)} copy(bf16[1,128,8192]{2,1,0:T(8,128)(2,1)S(1)} %bitcast.7) | data formatting | bytes 4194304
Async XLA Ops:
  108.0 2.4 %copy-start = (bf16[128,8192]{1,0:T(8,128)(2,1)S(1)}, bf16[128,8192]{1,0:T(8,128)(2,1)}, u32[]{:S(2)}) copy-start(bf16[128,8192]{1,0:T(8,128)(2,1)} %get-tuple-element.5) | copy-start | bytes 6291460

commit v4 on v3

--- a/solution.py
+++ b/solution.py
@@ -20,6 +20,8 @@
 RG = BLOCK // SUB
 MASKED = -1e30
 MIX = 13
+EARLY = 6
+PARTS = 2
 HALVES = 2
 KEYS = 384
 MESH = pl.DeviceIdType.MESH
@@ -35,8 +37,8 @@
 
 def kernel(
     n, sections, lens_hbm, plan_hbm, q_hbm, k_hbm, v_hbm, o_hbm, w_hbm, dq_hbm, out_hbm,
-    lens, plan, inv, q_s, o_s, dq_s, kvw, hold, send2, bias, s_s, g_s, part, terms, sums, totals, kvo, xbuf, blk, wsh, wfull, outs,
-    in_sem, kv_sem, dq_sem, s1s, s1r, g1s, g1r, s2s, s2r, s3s, s3r, rs, rr, xs, xr, ds_, dr, gs, gr, os_, or_, own_sem, loc_sem, wxs, wxr, wgs, wgr,
+    lens, plan, inv, q_s, o_s, dq_s, kvw, hold, send2, bias, s_s, g_s, part, terms, sums, totals, kvo, blk, wsh, wfull, outs,
+    in_sem, kv_sem, dq_sem, s1s, s1r, g1s, g1r, s2s, s2r, s3s, s3r, rs, rr, ds_, dr, gs, gr, os_, or_, own_terms, own_sem, ready, loc_sem, wxs, wxr, wgs, wgr,
 ):
     me = lax.axis_index("ctx")
     sec = lax.axis_index("section")
@@ -85,7 +87,9 @@
     for k in range(1, RG):
         for there in range(2):
             greet(device(rem(rg + k, RG), column, there))
-    pl.semaphore_signal(barrier, inc=1, device_id={"section": rem(sec + 1, sections)}, device_id_type=MESH)
+    after = rem(sec + 1, sections)
+    for neighbour in (before, after):
+        pl.semaphore_signal(barrier, inc=1, device_id={"section": neighbour}, device_id_type=MESH)
     load_plan.wait()
     load_lens.wait()
 
@@ -100,7 +104,8 @@
     lax.fori_loop(0, n, invert, 0)
     for load in load_kv:
         load.wait()
-    pl.semaphore_wait(barrier, CH - 1 + 2 * (RG - 1) + 1)
+    pl.semaphore_wait(barrier, CH - 1 + 2 * (RG - 1) + 2)
+    pl.semaphore_signal(ready, inc=1, device_id={"section": after}, device_id_type=MESH)
 
     def held_head(m):
         return rem(div(m, 2) + 2 * rem(m, 2), HK)
@@ -127,7 +132,10 @@
             for kind in range(2):
                 body(kind, rem(line[kind] + 3 * k, CH))
 
-    mates(lambda kind, m: piece_out(kind, m).start())
+    for far in (0, 1, 3, 2):
+        for there in ((1,) if far == 0 else (0, 1)):
+            for kind in range(2):
+                piece_out(kind, 2 * rem((rg if kind else column) + far, RG) + rem(core + there, 2)).start()
     w_shift = remote(w_hbm, wsh, wxs, wxr, section=before)
     w_shift.start()
     for kind in range(2):
@@ -146,26 +154,38 @@
     for kind in range(2):
         terms[kind, CH] = jnp.zeros((SLOTS, halves, HD), jnp.bfloat16)
 
-    def group(kind, i):
-        across_lines = rg if kind == 0 else column
-        return hold.at[kind, pl.ds(pl.multiple_of(rem(across_lines + i, RG) * CH, CH), CH)]
+    def pair(kind, i, far):
+        here, along_it = (rg, column) if kind == 0 else (column, rg)
+        first = rem(here + i, RG) * CH + 2 * rem(along_it + far, RG)
+        return hold.at[kind, pl.ds(pl.multiple_of(first, 2), 2)]
 
     def peer(kind, i):
         return device(rem(rg + i, RG), column, core) if kind == 0 else device(rg, rem(column + i, RG), core)
 
-    def group_out(kind, i):
-        return remote(group(kind, 0), group(kind, 0), g1s.at[kind, i], g1r.at[kind, RG - i], ctx=peer(kind, i))
-
-    def group_in(kind, i):
-        return remote(group(kind, i), group(kind, i), g1s.at[kind, i], g1r.at[kind, i], ctx=peer(kind, i))
-
-    mates(lambda kind, m: piece_in(kind, m).wait_recv())
-    for i in (1, 3, 2):
+    def pair_out(kind, i, far):
+        return remote(
+            pair(kind, 0, far), pair(kind, 0, far), g1s.at[kind, i, far], g1r.at[kind, RG - i, far], ctx=peer(kind, i)
+        )
+
+    def pair_in(kind, i, far):
+        return remote(
+            pair(kind, i, far), pair(kind, i, far), g1s.at[kind, i, far], g1r.at[kind, i, far], ctx=peer(kind, i)
+        )
+
+    def came_from(kind, far, there):
+        return 2 * rem((column if kind == 0 else rg) + far, RG) + there
+
+    for far in (0, 1, 3, 2):
         for kind in range(2):
-            group_out(kind, i).start()
-    for i in (1, 3, 2):
-        for kind in range(2):
-            group_in(kind, i).wait_recv()
+            if far:
+                piece_in(kind, came_from(kind, far, core)).wait_recv()
+            piece_in(kind, came_from(kind, far, 1 - core)).wait_recv()
+            for i in (1, 3, 2):
+                pair_out(kind, i, far).start()
+    for far in (0, 1, 3, 2):
+        for i in (1, 3, 2):
+            for kind in range(2):
+                pair_in(kind, i, far).wait_recv()
 
     def window_slots(kind, m):
         return kvw.at[kind * HK + held_head(m), pl.ds(0, BACK), half_of(m)]
@@ -242,20 +262,37 @@
     nt = (((1,), (1,)), ((), ()))
     tn = (((0,), (0,)), ((), ()))
 
-    def term_out(kind, m):
-        return remote(
-            part.at[kind * HK + held_head(m), :, half_of(m)], terms.at[kind, line[kind]],
-            s3s.at[kind, m], s3r.at[kind, line[kind]], ctx=mate(kind, m),
-        )
-
-    def term_own(kind):
+    cuts = (pl.ds(0, EARLY), pl.ds(EARLY, SLOTS - EARLY))
+
+    def term_out(kind, m, cut):
+        return remote(
+            part.at[kind * HK + held_head(m), cuts[cut], half_of(m)], terms.at[kind, line[kind], cuts[cut]],
+            s3s.at[kind, m, cut], s3r.at[kind, line[kind], cut], ctx=mate(kind, m),
+        )
+
+    def term_own(kind, cut):
         m = line[kind]
-        return pltpu.make_async_copy(part.at[kind * HK + held_head(m), :, half_of(m)], terms.at[kind, m], loc_sem.at[2 + 3 * kind])
-
-    def term_in(kind, m):
-        return remote(
-            part.at[0, :, half_of(0)], terms.at[kind, m], s3s.at[kind, m], s3r.at[kind, m], ctx=mate(kind, m)
-        )
+        return pltpu.make_async_copy(
+            part.at[kind * HK + held_head(m), cuts[cut], half_of(m)], terms.at[kind, m, cuts[cut]], own_terms.at[kind, cut]
+        )
+
+    def term_in(kind, m, cut):
+        return remote(
+            part.at[0, cuts[cut], half_of(0)], terms.at[kind, m, cuts[cut]],
+            s3s.at[kind, m, cut], s3r.at[kind, m, cut], ctx=mate(kind, m),
+        )
+
+    def send_terms(head, cut):
+        for half in range(2):
+            m = 2 * rem(head + RG - 2 * half, RG) + half
+            for kind in range(2):
+                @pl.when(m != line[kind])
+                def _():
+                    term_out(kind, m, cut).start()
+
+                @pl.when(m == line[kind])
+                def _():
+                    term_own(kind, cut).start()
 
     def one_head(step, carry):
         head = rem(step + turn_of, HK)
@@ -317,103 +354,95 @@
             part[head, slots] = dk.astype(jnp.bfloat16).reshape(KEYS // BLOCK, BLOCK, HD)
             keys = kvw[head, slots].reshape(KEYS, HD)
             dq = dq + lax.dot_general(score_low, keys, tn, preferred_element_type=jnp.float32)
+            if slots.stop == EARLY:
+                send_terms(head, 0)
         for i in range(GROUP):
             dq_s[:, columns(i)] = (dq[i * BLOCK:(i + 1) * BLOCK] * scale).astype(jnp.bfloat16)
 
-        for half in range(2):
-            m = 2 * rem(head + RG - 2 * half, RG) + half
-            for kind in range(2):
-                @pl.when(m != line[kind])
-                def _():
-                    term_out(kind, m).start()
-
-                @pl.when(m == line[kind])
-                def _():
-                    term_own(kind).start()
-
+        send_terms(head, 1)
         wide = pl.ds(pl.multiple_of(head * GROUP * HD, GROUP * HD), GROUP * HD)
         pltpu.make_async_copy(dq_s.at[:, wide], dq_hbm.at[:, wide], dq_sem.at[head]).start()
         return carry
 
     lax.fori_loop(0, HK, one_head, 0)
 
-    mates(lambda kind, m: term_in(kind, m).wait_recv())
-    for kind in range(2):
-        term_own(kind).wait()
-
-    def total_out(kind, i):
+    for cut in range(2):
+        mates(lambda kind, m: term_in(kind, m, cut).wait_recv())
+        for kind in range(2):
+            term_own(kind, cut).wait()
+
+    step_of = CH // PARTS
+
+    def some(first, part_no):
+        return pl.ds(pl.multiple_of(first * CH + part_no * step_of, step_of), step_of)
+
+    def total_out(kind, i, c):
         to = rem((rg if kind == 0 else column) + i, RG)
         return remote(
-            sums.at[kind, pl.ds(pl.multiple_of(to * CH, CH), CH)], totals.at[kind, RG - i],
-            rs.at[kind, i], rr.at[kind, RG - i], ctx=peer(kind, i),
-        )
-
-    def total_in(kind, i):
-        return remote(
-            sums.at[kind, pl.ds(0, CH)], totals.at[kind, i], rs.at[kind, i], rr.at[kind, i], ctx=peer(kind, i)
-        )
-
-    for i in (1, 2, 3, 0):
+            sums.at[kind, some(to, c)], totals.at[kind, RG - i, some(0, c)],
+            rs.at[kind, i, c], rr.at[kind, RG - i, c], ctx=peer(kind, i),
+        )
+
+    def total_in(kind, i, c):
+        return remote(
+            sums.at[kind, some(0, c)], totals.at[kind, i, some(0, c)], rs.at[kind, i, c], rr.at[kind, i, c], ctx=peer(kind, i)
+        )
+
+    for c in range(PARTS):
+        for i in (1, 3, 2, 0):
+            for kind in range(2):
+                here = rg if kind == 0 else column
+                to = rem(here + i, RG)
+
+                def one_block(e, carry):
+                    p = device(to, div(e, 2), rem(e, 2)) if kind == 0 else device(div(e, 2), to, rem(e, 2))
+                    total = jnp.zeros((halves, HD), jnp.float32)
+                    for w in range(SLOTS):
+                        later = plan[p] + BACK - w
+                        source = inv[kind, jnp.minimum(later, n - 1)]
+                        wanted = jnp.logical_and(later < n, div(source, CH) == here)
+                        total = total + terms[kind, jnp.where(wanted, rem(source, CH), CH), w].astype(jnp.float32)
+                    sums[kind, to * CH + e] = total.astype(jnp.bfloat16)
+                    return carry
+
+                lax.fori_loop(c * step_of, (c + 1) * step_of, one_block, 0)
+                if i > 0:
+                    total_out(kind, i, c).start()
+
+    def owned(kind, m):
+        return blk.at[0, 0, kind * HK + held_head(m), half_of(m)]
+
+    def deliver(kind, m):
+        return remote(
+            kvo.at[kind, m], owned(kind, line[kind]), ds_.at[kind, m], dr.at[kind, line[kind]],
+            section=before, ctx=mate(kind, m),
+        )
+
+    def delivered(kind, m):
+        return remote(kvo.at[kind, m], owned(kind, m), ds_.at[kind, m], dr.at[kind, m], section=before, ctx=mate(kind, m))
+
+    pl.semaphore_wait(ready, 1)
+    for c in range(PARTS):
         for kind in range(2):
             here = rg if kind == 0 else column
-            to = rem(here + i, RG)
-
-            def one_block(e, carry):
-                p = device(to, div(e, 2), rem(e, 2)) if kind == 0 else device(div(e, 2), to, rem(e, 2))
-                total = jnp.zeros((halves, HD), jnp.float32)
-                for w in range(SLOTS):
-                    later = plan[p] + BACK - w
-                    source = inv[kind, jnp.minimum(later, n - 1)]
-                    wanted = jnp.logical_and(later < n, div(source, CH) == here)
-                    total = total + terms[kind, jnp.where(wanted, rem(source, CH), CH), w].astype(jnp.float32)
-                sums[kind, to * CH + e] = total.astype(jnp.bfloat16)
+            for i in range(1, RG):
+                total_in(kind, i, c).wait_recv()
+
+            def one_sum(e, carry):
+                total = sums[kind, here * CH + c * step_of + e].astype(jnp.float32)
+                for i in range(1, RG):
+                    total = total + totals[kind, i, c * step_of + e].astype(jnp.float32)
+                kvo[kind, c * step_of + e] = total.astype(jnp.bfloat16)
                 return carry
 
-            lax.fori_loop(0, CH, one_block, 0)
-            if i > 0:
-                total_out(kind, i).start()
-
-    def x_copy(kind):
-        return remote(kvo.at[kind], xbuf.at[kind], xs.at[kind], xr.at[kind], section=before)
-
-    for kind in range(2):
-        here = rg if kind == 0 else column
-        for i in range(1, RG):
-            total_in(kind, i).wait_recv()
-
-        def one_sum(e, carry):
-            total = sums[kind, here * CH + e].astype(jnp.float32)
-            for i in range(1, RG):
-                total = total + totals[kind, i, e].astype(jnp.float32)
-            kvo[kind, e] = total.astype(jnp.bfloat16)
-            return carry
-
-        lax.fori_loop(0, CH, one_sum, 0)
-        x_copy(kind).start()
-
-    def owned(kind, m):
-        return blk.at[0, 0, kind * HK + held_head(m), half_of(m)]
-
-    def deliver(kind, m):
-        return remote(
-            xbuf.at[kind, m], owned(kind, line[kind]), ds_.at[kind, m], dr.at[kind, line[kind]], ctx=mate(kind, m)
-        )
-
-    def deliver_own(kind):
-        return pltpu.make_async_copy(xbuf.at[kind, line[kind]], owned(kind, line[kind]), loc_sem.at[3 + 3 * kind])
-
-    def delivered(kind, m):
-        return remote(xbuf.at[kind, m], owned(kind, m), ds_.at[kind, m], dr.at[kind, m], ctx=mate(kind, m))
-
-    for kind in range(2):
-        x_copy(kind).wait_recv()
-        for k in range(1, CH):
-            deliver(kind, rem(line[kind] + 3 * k, CH)).start()
-        deliver_own(kind).start()
-
-    mates(lambda kind, m: delivered(kind, m).wait_recv())
-    for kind in range(2):
-        deliver_own(kind).wait()
+            lax.fori_loop(0, step_of, one_sum, 0)
+        for e in range(step_of):
+            for kind in range(2):
+                deliver(kind, c * step_of + rem(e + line[kind], step_of)).start()
+
+    for m in range(CH):
+        for kind in range(2):
+            delivered(kind, m).wait_recv()
 
     sibling = device(rg, column, 1 - core)
     half = BLOCK // HALVES
@@ -538,15 +567,18 @@
 
     mates(lambda kind, m: piece_out(kind, m).wait_send())
     mates(lambda kind, m: window_out(kind, m).wait_send())
-    for i in range(1, RG):
-        for kind in range(2):
-            group_out(kind, i).wait_send()
-    mates(lambda kind, m: term_out(kind, m).wait_send())
-    mates(lambda kind, m: deliver(kind, m).wait_send())
+    for far in range(RG):
+        for i in range(1, RG):
+            for kind in range(2):
+                pair_out(kind, i, far).wait_send()
+    for cut in range(2):
+        mates(lambda kind, m: term_out(kind, m, cut).wait_send())
     for kind in range(2):
-        x_copy(kind).wait_send()
-        for i in range(1, RG):
-            total_out(kind, i).wait_send()
+        for m in range(CH):
+            deliver(kind, m).wait_send()
+        for c in range(PARTS):
+            for i in range(1, RG):
+                total_out(kind, i, c).wait_send()
     w_shift.wait_send()
     for z in range(RG):
         @pl.when(w_target(z) != me)
@@ -626,17 +658,17 @@
             pltpu.VMEM((2, n, BLOCK // 2, HD), low),
             pltpu.VMEM((2, RG, CH, BLOCK // 2, HD), low),
             pltpu.VMEM((2, CH, BLOCK // 2, HD), low),
-            pltpu.VMEM((2, CH, BLOCK // 2, HD), low),
             pltpu.VMEM((7, 2, CH, BLOCK, HD), low),
             pltpu.VMEM((features, CH * HD), low),
             pltpu.VMEM((share, CH * HD), low),
             pltpu.VMEM((HALVES, 2, RG, 2, 2, BLOCK // HALVES, features), low),
             dma((4,)), dma((2, HK)), dma((HK,)),
-            dma((2, CH)), dma((2, CH)), dma((2, RG)), dma((2, RG)), dma((2, CH)), dma((2, CH)), dma((2, CH)), dma((2, CH)),
-            dma((2, RG)), dma((2, RG)), dma((2,)), dma((2,)), dma((2, CH)), dma((2, CH)),
+            dma((2, CH)), dma((2, CH)), dma((2, RG, RG)), dma((2, RG, RG)), dma((2, CH)), dma((2, CH)),
+            dma((2, CH, 2)), dma((2, CH, 2)),
+            dma((2, RG, PARTS)), dma((2, RG, PARTS)), dma((2, CH)), dma((2, CH)),
             dma((HALVES, 14)), dma((HALVES, 7, 2)),
-            dma((HALVES, 2, RG, 2, 2)), dma((HALVES, 2, RG, 2, 2)), dma((HALVES, 2, 2)),
-            dma((7,)), dma, dma, dma((RG,)), dma((RG,)),
+            dma((HALVES, 2, RG, 2, 2)), dma((HALVES, 2, RG, 2, 2)), dma((2, 2)), dma((HALVES, 2, 2)),
+            pltpu.SemaphoreType.REGULAR, dma((7,)), dma, dma, dma((RG,)), dma((RG,)),
         ],
         compiler_params=pltpu.CompilerParams(
             collective_id=0, has_side_effects=True, vmem_limit_bytes=56 * 1024 * 1024

time: 112 us -> 107 us (0.955)
  Pallas kernels: 107 us -> 102 us
    pallas_call x1, Pallas kernels: 107 us -> 102 us  [shards(): pl.pallas_call(functools.partial(kernel, n, sections), out_shape=(jax.Sha...]
where the time goes in v4:
time: 107 us
  Pallas kernels  102 us (95%)
  local copies, waits for them, and re-layouts  3.76 us (4%)
    pallas_call x1, Pallas kernels, shards(): pl.pallas_call(functools.partial(kernel, n, sections), out_shape=(jax.Sha...  102 us
    unnamed x4, local copies, waits for them, and re-layouts  3.76 us

profile of v4, /device:TPU:1, one launch (start us, length us, event | category | flops | bytes accessed | tf_op | source)
XLA Modules:
  0.0 106.8 jit_solution(17234388892151654604)
XLA Ops:
  0.6 102.4 %shard_map.86 = (bf16[128,4096]{1,0:T(8,128)(2,1)}, bf16[128,8192]{1,0:T(8,128)(2,1)}) custom-call(s32[16]{0:T(128)} %lens_hbm.1, s32[32]{0:T(128)} %plan_hbm.1, bf16[128,4096]{1,0:T(8,128)(2,1)} %bitcast.8, bf16[128,512]{1,0:T(8,128)(2,1)} %bitcast.12, bf16[128,512]{1,0:T(8,128)(2,1)} %bitcast.13, bf16[128,4096]{1,0:T(8,128)(2,1)} %bitcast.9, ...), custom_call_target="tpu_custom_call" | custom-call | tf_op jit(solution)/shard_map/pallas_call | solution.py:635
  103.0 0.0 copy-start
  103.0 2.4 %copy.11 = bf16[1,128,4096]{2,1,0:T(8,128)(2,1)} copy(bf16[1,128,4096]{2,1,0:T(8,128)(2,1)} %bitcast.10) | data formatting | bytes 2097152
  105.4 0.0 copy-done
  105.4 1.3 %copy.12 = bf16[1,128,8192]{2,1,0:T(8,128)(2,1)} copy(bf16[1,128,8192]{2,1,0:T(8,128)(2,1)S(1)} %bitcast.7) | data formatting | bytes 4194304
Async XLA Ops:
  103.0 2.4 %copy-start = (bf16[128,8192]{1,0:T(8,128)(2,1)S(1)}, bf16[128,8192]{1,0:T(8,128)(2,1)}, u32[]{:S(2)}) copy-start(bf16[128,8192]{1,0:T(8,128)(2,1)} %get-tuple-element.5) | copy-start | bytes 6291460

commit v5 on v4

--- a/solution.py
+++ b/solution.py
@@ -307,7 +307,7 @@
                 def _():
                     window_own(kind).wait()
 
-        @pl.when(step == 1)
+        @pl.when(step == 0)
         def _():
             spread_weights()
 
@@ -331,8 +331,6 @@
             s_s[span] = scores
             top = folded(scores, jnp.max)
             peak = top if peak is None else jnp.maximum(peak, top)
-            values = kvw[HK + head, slots].reshape(KEYS, HD)
-            g_s[span] = lax.dot_general(values, o2, nt, preferred_element_type=jnp.float32)
         peak = jnp.max(peak, axis=0, keepdims=True)
         total = jnp.zeros((8, wide), jnp.float32)
         weighted = jnp.zeros((8, wide), jnp.float32)
@@ -340,7 +338,10 @@
             terms = jnp.exp2((s_s[span] - peak) * power)
             s_s[span] = terms
             total = total + folded(terms, jnp.sum)
-            weighted = weighted + folded(terms * g_s[span], jnp.sum)
+            values = kvw[HK + head, slots].reshape(KEYS, HD)
+            grads = lax.dot_general(values, o2, nt, preferred_element_type=jnp.float32)
+            g_s[span] = grads
+            weighted = weighted + folded(terms * grads, jnp.sum)
         inverse = 1.0 / jnp.sum(total, axis=0, keepdims=True)
         delta = jnp.sum(weighted, axis=0, keepdims=True) * inverse
         dq = jnp.zeros((wide, HD), jnp.float32)
@@ -389,7 +390,7 @@
         )
 
     for c in range(PARTS):
-        for i in (1, 3, 2, 0):
+        for i in (2, 1, 3, 0):
             for kind in range(2):
                 here = rg if kind == 0 else column
                 to = rem(here + i, RG)

time: 107 us -> 105 us (0.981)
  Pallas kernels: 102 us -> 100 us
    pallas_call x1, Pallas kernels: 102 us -> 100 us  [shards(): pl.pallas_call(functools.partial(kernel, n, sections), out_shape=(jax.Sha...]
where the time goes in v5:
time: 105 us
  Pallas kernels  100 us (95%)
  local copies, waits for them, and re-layouts  3.76 us (4%)
    pallas_call x1, Pallas kernels, shards(): pl.pallas_call(functools.partial(kernel, n, sections), out_shape=(jax.Sha...  100 us
    unnamed x4, local copies, waits for them, and re-layouts  3.76 us

profile of v5, /device:TPU:1, one launch (start us, length us, event | category | flops | bytes accessed | tf_op | source)
XLA Modules:
  0.0 104.5 jit_solution(3996159637013049722)
XLA Ops:
  0.6 100.1 %shard_map.86 = (bf16[128,4096]{1,0:T(8,128)(2,1)}, bf16[128,8192]{1,0:T(8,128)(2,1)}) custom-call(s32[16]{0:T(128)} %lens_hbm.1, s32[32]{0:T(128)} %plan_hbm.1, bf16[128,4096]{1,0:T(8,128)(2,1)} %bitcast.8, bf16[128,512]{1,0:T(8,128)(2,1)} %bitcast.12, bf16[128,512]{1,0:T(8,128)(2,1)} %bitcast.13, bf16[128,4096]{1,0:T(8,128)(2,1)} %bitcast.9, ...), custom_call_target="tpu_custom_call" | custom-call | tf_op jit(solution)/shard_map/pallas_call | solution.py:636
  100.7 0.0 copy-start
  100.7 2.4 %copy.11 = bf16[1,128,4096]{2,1,0:T(8,128)(2,1)} copy(bf16[1,128,4096]{2,1,0:T(8,128)(2,1)} %bitcast.10) | data formatting | bytes 2097152
  103.2 0.0 copy-done
  103.2 1.3 %copy.12 = bf16[1,128,8192]{2,1,0:T(8,128)(2,1)} copy(bf16[1,128,8192]{2,1,0:T(8,128)(2,1)S(1)} %bitcast.7) | data formatting | bytes 4194304
Async XLA Ops:
  100.7 2.4 %copy-start = (bf16[128,8192]{1,0:T(8,128)(2,1)S(1)}, bf16[128,8192]{1,0:T(8,128)(2,1)}, u32[]{:S(2)}) copy-start(bf16[128,8192]{1,0:T(8,128)(2,1)} %get-tuple-element.5) | copy-start | bytes 6291460

commit v6 on v5

--- a/solution.py
+++ b/solution.py
@@ -306,10 +306,6 @@
                 @pl.when(m == line[kind])
                 def _():
                     window_own(kind).wait()
-
-        @pl.when(step == 0)
-        def _():
-            spread_weights()
 
         def columns(i):
             return pl.ds(pl.multiple_of((head * GROUP + i) * HD, HD), HD)
@@ -365,6 +361,7 @@
         pltpu.make_async_copy(dq_s.at[:, wide], dq_hbm.at[:, wide], dq_sem.at[head]).start()
         return carry
 
+    spread_weights()
     lax.fori_loop(0, HK, one_head, 0)
 
     for cut in range(2):

time: 105 us -> 104 us (level)
    pallas_call x1, Pallas kernels: 100 us -> 99 us  [shards(): pl.pallas_call(functools.partial(kernel, n, sections), out_shape=(jax.Sha...]
where the time goes in v6:
time: 104 us; the launch traced here: 103 us
  Pallas kernels  99 us (95%)
  local copies, waits for them, and re-layouts  3.76 us (4%)
    pallas_call x1, Pallas kernels, shards(): pl.pallas_call(functools.partial(kernel, n, sections), out_shape=(jax.Sha...  99 us
    unnamed x4, local copies, waits for them, and re-layouts  3.76 us

profile of v6, /device:TPU:1, one launch (start us, length us, event | category | flops | bytes accessed | tf_op | source)
XLA Modules:
  0.0 103.4 jit_solution(663190471124854631)
XLA Ops:
  0.6 99.0 %shard_map.86 = (bf16[128,4096]{1,0:T(8,128)(2,1)}, bf16[128,8192]{1,0:T(8,128)(2,1)}) custom-call(s32[16]{0:T(128)} %lens_hbm.1, s32[32]{0:T(128)} %plan_hbm.1, bf16[128,4096]{1,0:T(8,128)(2,1)} %bitcast.8, bf16[128,512]{1,0:T(8,128)(2,1)} %bitcast.12, bf16[128,512]{1,0:T(8,128)(2,1)} %bitcast.13, bf16[128,4096]{1,0:T(8,128)(2,1)} %bitcast.9, ...), custom_call_target="tpu_custom_call" | custom-call | tf_op jit(solution)/shard_map/pallas_call | solution.py:633
  99.6 0.0 copy-start
  99.6 2.4 %copy.11 = bf16[1,128,4096]{2,1,0:T(8,128)(2,1)} copy(bf16[1,128,4096]{2,1,0:T(8,128)(2,1)} %bitcast.10) | data formatting | bytes 2097152
  102.1 0.0 copy-done
  102.1 1.3 %copy.12 = bf16[1,128,8192]{2,1,0:T(8,128)(2,1)} copy(bf16[1,128,8192]{2,1,0:T(8,128)(2,1)S(1)} %bitcast.7) | data formatting | bytes 4194304
Async XLA Ops:
  99.6 2.4 %copy-start = (bf16[128,8192]{1,0:T(8,128)(2,1)S(1)}, bf16[128,8192]{1,0:T(8,128)(2,1)}, u32[]{:S(2)}) copy-start(bf16[128,8192]{1,0:T(8,128)(2,1)} %get-tuple-element.5) | copy-start | bytes 6291460
